TPU v7x, 32 devices: a whole 2x2x4 slice. The times are simulated.
32 devices in a mesh: dom: 8 (over z, core), feat: 4 (over y, x).
Axes of the slice: x: 2, y: 2, z: 4, core: 2. Of those that a mesh axis runs over, the one named last changes fastest.
Arguments:
- features_t: bfloat16 [256, 12288], P('feat', 'dom'), may hold values from -6 to 6
- weight: bfloat16 [256, 256], P(None, 'feat'), may hold values from -0.375 to 0.375
- tile_values: bfloat16 [8, 4, 16, 128, 128], P('dom'), may hold values from -0.21875 to 0.21875
- row_tiles: int32 [8, 4, 16], P('dom'), may hold values from 0 to 11
- col_tiles: int32 [8, 4, 16], P('dom'), may hold values from 0 to 11
- tile_counts: int32 [8, 4], P('dom'), may hold values from 1 to 16
- cotangent_t: bfloat16 [256, 12288], P('feat', 'dom'), may hold values from -6 to 6
Outputs:
- output_t: bfloat16 [256, 12288], P('feat', 'dom')
- weight_grad: float32 [256, 256], P(None, 'feat')
- feature_grad_t: bfloat16 [256, 12288], P('feat', 'dom')
Inputs may be any that keep to these rules, and one draw needn't show every extreme that they name: Tile pairs may repeat.
All inputs are finite; a program needn't handle non-finite values.
Results may differ from a plain program's by a relative error of at most 0.011.
Values may be sent and summed in bfloat16 or wider, within the bound.
A program may use at most 64 MiB of HBM per device.

v0:
```python
import math

import jax
import jax.numpy as jnp
from jax import lax
from jax.sharding import PartitionSpec as P


def shifted(block, axis, distance):
    devices = range(lax.axis_size(axis))
    route = [((i - distance) % len(devices), i) for i in devices]
    return lax.ppermute(block, axis, route)


def masked_table(indices, used_slots, table_size):
    slots = jnp.arange(indices.shape[0], dtype=jnp.int32)
    valid = (slots < used_slots).astype(jnp.float32)
    table = (indices[:, None] == jnp.arange(table_size, dtype=jnp.int32)[None, :]).astype(
        jnp.float32
    )
    return table * valid[:, None]


def body(features_t, weight, tile_values, row_tiles, col_tiles, tile_counts, cotangent_t):
    width, node_rows = features_t.shape
    step_count = tile_values.shape[1]
    tile_side = tile_values.shape[3]
    tiles_per = node_rows // tile_side
    values = tile_values[0]
    row_index = row_tiles[0]
    col_index = col_tiles[0]
    counts = tile_counts[0]

    def forward_piece(feat_block, step_index):
        blocks = feat_block.reshape(width, tiles_per, tile_side)
        picked = jnp.take(blocks, col_index[step_index], axis=1)
        products = jnp.einsum(
            "fkc,krc->fkr", picked, values[step_index], preferred_element_type=jnp.float32
        )
        scatter_table = masked_table(row_index[step_index], counts[step_index], tiles_per)
        return jnp.einsum("fkr,kt->ftr", products, scatter_table).reshape(width, node_rows)

    def advance(step_index, loop_state):
        feat_block, running = loop_state
        feat_block = shifted(feat_block, "dom", 1)
        return (feat_block, running + forward_piece(feat_block, step_index))

    _, hidden_sum = lax.fori_loop(
        1, step_count, advance, (features_t, forward_piece(features_t, 0))
    )
    hidden_t = hidden_sum.astype(jnp.bfloat16)
    slab_piece = lax.all_gather(hidden_t, "feat", axis=0, tiled=True)
    weight_rows = weight
    output_acc = lax.dot_general(
        weight_rows, slab_piece, (((0,), (0,)), ((), ())), preferred_element_type=jnp.float32
    )
    grad_part = lax.dot_general(
        slab_piece, cotangent_t, (((1,), (1,)), ((), ())), preferred_element_type=jnp.float32
    )
    output_acc, grad_local = (output_acc, grad_part)
    grad_scale = 1.0 / math.sqrt(node_rows * lax.axis_size("dom"))
    weight_grad = lax.psum(grad_local, "dom") * grad_scale
    weight_rows = weight
    grad_hidden = lax.psum_scatter(
        jnp.dot(weight_rows, cotangent_t, preferred_element_type=jnp.float32),
        "feat",
        scatter_dimension=0,
        tiled=True,
    ).astype(jnp.bfloat16)

    def backward_piece(step_index):
        blocks = grad_hidden.reshape(width, tiles_per, tile_side)
        picked = jnp.take(blocks, row_index[step_index], axis=1)
        products = jnp.einsum(
            "fkr,krc->fkc", picked, values[step_index], preferred_element_type=jnp.float32
        )
        scatter_table = masked_table(col_index[step_index], counts[step_index], tiles_per)
        return jnp.einsum("fkc,kt->ftc", products, scatter_table).reshape(width, node_rows)

    def retreat(loop_index, running):
        step_index = step_count - 2 - loop_index
        return shifted(running, "dom", -1) + backward_piece(step_index)

    grad_sum = lax.fori_loop(0, step_count - 1, retreat, backward_piece(step_count - 1))
    feature_grad_t = grad_sum.astype(jnp.bfloat16)
    return (output_acc.astype(jnp.bfloat16), weight_grad, feature_grad_t)


def solution(mesh):
    in_specs = (
        P("feat", "dom"),
        P(None, "feat"),
        P("dom", None, None, None, None),
        P("dom", None, None),
        P("dom", None, None),
        P("dom", None),
        P("feat", "dom"),
    )
    out_specs = (P("feat", "dom"), P(None, "feat"), P("feat", "dom"))
    return jax.shard_map(body, mesh=mesh, in_specs=in_specs, out_specs=out_specs, check_vma=False)
```

profile of v0, /device:TPU:0, one launch (start us, length us, event | category | flops | bytes accessed | tf_op | source)
XLA Modules:
  0.0 145.1 jit_solution(10513631939833939001)
XLA Ops:
  8.1 1.1 copy.81
  9.9 1.3 fusion.75
  13.2 1.5 %fusion.47 = bf16[16,64,128]{2,1,0:T(8,128)(2,1)S(1)} fusion(bf16[1,4,16,128,128]{4,3,2,1,0:T(8,128)(2,1)} %param.15, bf16[16,64,128]{2,1,0:T(8,128)(2,1)S(1)} %gather_fusion.2, pred[16]{0:T(512)(128)(4,1)S(1)} %get-tuple-element.392), kind=kOutput, calls=%fused_computation.70 | convolution fusion | flops 33685504 | bytes 1048592 | tf_op jit(solution)/shard_map/fkc,krc->fkr/dot_general | solution.py:37
  15.2 26.8 %while.32 = (s32[]{:T(128)}, bf16[64,1536]{1,0:T(8,128)(2,1)S(1)}, f32[64,1536]{1,0:T(8,128)S(1)}, s32[4,16]{1,0:T(4,128)S(1)}, s32[4]{0:T(128)S(1)}, /*index=5*...) while((s32[]{:T(128)}, bf16[64,1536]{1,0:T(8,128)(2,1)S(1)}, ...), condition=%wide.region_1.3_spmd, body=%wide.region_0.0_spmd.sunk | while | flops 36931076 | bytes 4986083 | solution.py:48
  17.0 6.1 %collective-permute-done = bf16[64,1536]{1,0:T(8,128)(2,1)S(1)} collective-permute-done((bf16[64,1536]{1,0:T(8,128)(2,1)S(1)}, bf16[64,1536]{1,0:T(8,128)(2,1)S(1)}, u32[]{:S(2)}, u32[]{:S(2)}) %collective-permute-start) | collective-permute-done | bytes 196640 | tf_op jit(solution)/shard_map/while/body/eval_jaxpr/ppermute | solution.py:12
  26.1 5.6 %collective-permute-done = bf16[64,1536]{1,0:T(8,128)(2,1)S(1)} collective-permute-done((bf16[64,1536]{1,0:T(8,128)(2,1)S(1)}, bf16[64,1536]{1,0:T(8,128)(2,1)S(1)}, u32[]{:S(2)}, u32[]{:S(2)}) %collective-permute-start) | collective-permute-done | bytes 196640 | tf_op jit(solution)/shard_map/while/body/eval_jaxpr/ppermute | solution.py:12
  34.7 5.6 %collective-permute-done = bf16[64,1536]{1,0:T(8,128)(2,1)S(1)} collective-permute-done((bf16[64,1536]{1,0:T(8,128)(2,1)S(1)}, bf16[64,1536]{1,0:T(8,128)(2,1)S(1)}, u32[]{:S(2)}, u32[]{:S(2)}) %collective-permute-start) | collective-permute-done | bytes 196640 | tf_op jit(solution)/shard_map/while/body/eval_jaxpr/ppermute | solution.py:12
  42.0 11.6 %all_gather.3 = bf16[256,1536]{1,0:T(8,128)(2,1)S(1)} all-gather(bf16[64,1536]{1,0:T(8,128)(2,1)S(1)} %convert_element_type.66), channel_id=1, replica_groups=mesh['dom'=8,'feat'=4] {'feat'}, dimensions={0}, use_global_device_ids=true | all-gather | bytes 983040 | tf_op jit(solution)/shard_map/all_gather | solution.py:52
  53.6 1.0 fusion.76
  54.7 1.6 %fusion.77 = f32[256,1536]{1,0:T(8,128)} fusion(bf16[256,64]{0,1:T(8,128)(2,1)S(1)} %copy-done.3, bf16[64,1536]{1,0:T(8,128)(2,1)S(1)} %copy-done), kind=kOutput, calls=%fused_computation.117 | convolution fusion | flops 50331648 | bytes 1802240 | tf_op jit(solution)/shard_map/dot_general | solution.py:65
  57.0 0.9 fusion.40
  57.9 47.7 %all-reduce.2.cloned.1.call-done = f32[256,64]{0,1:T(8,128)} async-done(((f32[256,64]{0,1:T(8,128)}), f32[256,64]{0,1:T(8,128)}) %all-reduce.2.cloned.1.call-update) | async-done | bytes 65552 | tf_op jit(solution)/shard_map/psum | solution.py:62
  105.6 1.5 %broadcast_multiply_fusion = f32[256,64]{0,1:T(8,128)} fusion(f32[256,64]{0,1:T(8,128)} %all-reduce.2.cloned.1.call-done), kind=kLoop, calls=%fused_computation.88 | loop fusion | flops 16384 | bytes 131072 | tf_op jit(solution)/shard_map/mul | solution.py:62
  107.1 1.1 copy_bitcast_fusion.4
  109.6 27.4 %while.33 = (s32[]{:T(128)}, f32[64,1536]{1,0:T(8,128)S(1)}, s32[4,16]{1,0:T(4,128)S(1)}, s32[4]{0:T(128)S(1)}, bf16[4,16,128,128]{3,2,1,0:T(8,128)(2,1)S(1)}, /...) while((s32[]{:T(128)}, f32[64,1536]{1,0:T(8,128)S(1)}, ...), condition=%wide.region_5.7_spmd, body=%wide.region_4.6_spmd.sunk | while | flops 36931076 | bytes 5379311 | solution.py:84
  112.4 2.8 %collective-permute-done.1 = f32[64,1536]{1,0:T(8,128)} collective-permute-done((f32[64,1536]{1,0:T(8,128)S(1)}, f32[64,1536]{1,0:T(8,128)}, u32[]{:S(2)}, u32[]{:S(2)}) %collective-permute-start.1) | collective-permute-done | bytes 393248 | tf_op jit(solution)/shard_map/while/body/eval_jaxpr/ppermute | solution.py:12
  115.1 1.2 bitcast_add_fusion.5
  116.3 3.9 %collective-permute-start.1 = (f32[64,1536]{1,0:T(8,128)S(1)}, f32[64,1536]{1,0:T(8,128)}, u32[]{:S(2)}, u32[]{:S(2)}) collective-permute-start(f32[64,1536]{1,0:T(8,128)S(1)} %get-tuple-element.532), channel_id=1, source_target_pairs={{4,0},{8,4},{12,8},{16,12},{20,16},{24,20},{28,24},{0,28},{5,1},{9... | collective-permute-start | bytes 1179656 | tf_op jit(solution)/shard_map/while/body/eval_jaxpr/ppermute | solution.py:12
  122.7 2.8 %collective-permute-done.1 = f32[64,1536]{1,0:T(8,128)} collective-permute-done((f32[64,1536]{1,0:T(8,128)S(1)}, f32[64,1536]{1,0:T(8,128)}, u32[]{:S(2)}, u32[]{:S(2)}) %collective-permute-start.1) | collective-permute-done | bytes 393248 | tf_op jit(solution)/shard_map/while/body/eval_jaxpr/ppermute | solution.py:12
  125.5 1.2 bitcast_add_fusion.5
  126.6 3.9 %collective-permute-start.1 = (f32[64,1536]{1,0:T(8,128)S(1)}, f32[64,1536]{1,0:T(8,128)}, u32[]{:S(2)}, u32[]{:S(2)}) collective-permute-start(f32[64,1536]{1,0:T(8,128)S(1)} %get-tuple-element.532), channel_id=1, source_target_pairs={{4,0},{8,4},{12,8},{16,12},{20,16},{24,20},{28,24},{0,28},{5,1},{9... | collective-permute-start | bytes 1179656 | tf_op jit(solution)/shard_map/while/body/eval_jaxpr/ppermute | solution.py:12
  133.0 2.8 %collective-permute-done.1 = f32[64,1536]{1,0:T(8,128)} collective-permute-done((f32[64,1536]{1,0:T(8,128)S(1)}, f32[64,1536]{1,0:T(8,128)}, u32[]{:S(2)}, u32[]{:S(2)}) %collective-permute-start.1) | collective-permute-done | bytes 393248 | tf_op jit(solution)/shard_map/while/body/eval_jaxpr/ppermute | solution.py:12
  135.8 1.2 bitcast_add_fusion.5
  137.0 0.7 convert_element_type.71
  (101 shorter events, 22.2 us)
Async XLA Ops:
  8.0 45.6 %copy-start = (bf16[64,1536]{1,0:T(8,128)(2,1)S(1)}, bf16[64,1536]{1,0:T(8,128)(2,1)}, u32[]{:S(2)}) copy-start(bf16[64,1536]{1,0:T(8,128)(2,1)} %param.19) | copy-start | bytes 589828
  8.0 7.1 %copy-start.1 = (bf16[1,4,16,128,128]{4,3,2,1,0:T(8,128)(2,1)S(1)}, bf16[1,4,16,128,128]{4,3,2,1,0:T(8,128)(2,1)}, u32[]{:S(2)}) copy-start(bf16[1,4,16,128,128]{4,3,2,1,0:T(8,128)(2,1)} %param.15) | copy-start | bytes 6291460
  8.0 7.1 %copy-start.5 = (s32[1,4,16]{2,1,0:T(4,128)S(1)}, s32[1,4,16]{2,1,0:T(4,128)}, u32[]{:S(2)}) copy-start(s32[1,4,16]{2,1,0:T(4,128)} %param.16) | copy-start | bytes 772
  8.0 7.1 %copy-start.4 = (s32[1,4,16]{2,1,0:T(4,128)S(1)}, s32[1,4,16]{2,1,0:T(4,128)}, u32[]{:S(2)}) copy-start(s32[1,4,16]{2,1,0:T(4,128)} %param.17) | copy-start | bytes 772
  8.0 7.1 %copy-start.6 = (s32[1,4]{1,0:T(1,128)S(1)}, s32[1,4]{1,0:T(1,128)}, u32[]{:S(2)}) copy-start(s32[1,4]{1,0:T(1,128)} %param.18) | copy-start | bytes 52
  8.1 97.6 %all-reduce.2.cloned.1.call-start = ((), (), s32[]{:S(2)}) async-start(), calls=%async_computation.1 | async-start | bytes 131072 | tf_op jit(solution)/shard_map/psum | solution.py:62
  15.2 7.9 %collective-permute-start = (bf16[64,1536]{1,0:T(8,128)(2,1)S(1)}, bf16[64,1536]{1,0:T(8,128)(2,1)S(1)}, u32[]{:S(2)}, u32[]{:S(2)}) collective-permute-start(bf16[64,1536]{1,0:T(8,128)(2,1)S(1)} %get-tuple-element.501), channel_id=1, source_target_pairs={{28,0},{0,4},{4,8},{8,12},{12,16},{16,20},{20,24},{24,28},{29,1},{... | collective-permute-start | bytes 589832 | tf_op jit(solution)/shard_map/while/body/eval_jaxpr/ppermute | solution.py:12
  24.7 6.9 %collective-permute-start = (bf16[64,1536]{1,0:T(8,128)(2,1)S(1)}, bf16[64,1536]{1,0:T(8,128)(2,1)S(1)}, u32[]{:S(2)}, u32[]{:S(2)}) collective-permute-start(bf16[64,1536]{1,0:T(8,128)(2,1)S(1)} %get-tuple-element.501), channel_id=1, source_target_pairs={{28,0},{0,4},{4,8},{8,12},{12,16},{16,20},{20,24},{24,28},{29,1},{... | collective-permute-start | bytes 589832 | tf_op jit(solution)/shard_map/while/body/eval_jaxpr/ppermute | solution.py:12
  33.3 6.9 %collective-permute-start = (bf16[64,1536]{1,0:T(8,128)(2,1)S(1)}, bf16[64,1536]{1,0:T(8,128)(2,1)S(1)}, u32[]{:S(2)}, u32[]{:S(2)}) collective-permute-start(bf16[64,1536]{1,0:T(8,128)(2,1)S(1)} %get-tuple-element.501), channel_id=1, source_target_pairs={{28,0},{0,4},{4,8},{8,12},{12,16},{16,20},{20,24},{24,28},{29,1},{... | collective-permute-start | bytes 589832 | tf_op jit(solution)/shard_map/while/body/eval_jaxpr/ppermute | solution.py:12
  42.0 12.7 %copy-start.3 = (bf16[256,64]{0,1:T(8,128)(2,1)S(1)}, bf16[256,64]{0,1:T(8,128)(2,1)}, u32[]{:S(2)}) copy-start(bf16[256,64]{0,1:T(8,128)(2,1)} %param.14) | copy-start | bytes 98308
  54.6 52.5 %reduce-scatter.2.cloned.1.call-start = ((), (), s32[]{:S(2)}) async-start(), calls=%async_computation.2 | async-start | bytes 1966080 | tf_op jit(solution)/shard_map/reduce_scatter | solution.py:64
  107.1 2.4 %copy-start.2 = (f32[64,1536]{1,0:T(8,128)S(1)}, f32[64,1536]{1,0:T(8,128)}, u32[]{:S(2)}) copy-start(f32[64,1536]{1,0:T(8,128)} %reduce-scatter.2.cloned.1.call-done) | copy-start | bytes 1179652
  109.6 5.5 %collective-permute-start.1 = (f32[64,1536]{1,0:T(8,128)S(1)}, f32[64,1536]{1,0:T(8,128)}, u32[]{:S(2)}, u32[]{:S(2)}) collective-permute-start(f32[64,1536]{1,0:T(8,128)S(1)} %get-tuple-element.532), channel_id=1, source_target_pairs={{4,0},{8,4},{12,8},{16,12},{20,16},{24,20},{28,24},{0,28},{5,1},{9... | collective-permute-start | bytes 1179656 | tf_op jit(solution)/shard_map/while/body/eval_jaxpr/ppermute | solution.py:12
  116.3 9.2 %collective-permute-start.1 = (f32[64,1536]{1,0:T(8,128)S(1)}, f32[64,1536]{1,0:T(8,128)}, u32[]{:S(2)}, u32[]{:S(2)}) collective-permute-start(f32[64,1536]{1,0:T(8,128)S(1)} %get-tuple-element.532), channel_id=1, source_target_pairs={{4,0},{8,4},{12,8},{16,12},{20,16},{24,20},{28,24},{0,28},{5,1},{9... | collective-permute-start | bytes 1179656 | tf_op jit(solution)/shard_map/while/body/eval_jaxpr/ppermute | solution.py:12
  126.6 9.2 %collective-permute-start.1 = (f32[64,1536]{1,0:T(8,128)S(1)}, f32[64,1536]{1,0:T(8,128)}, u32[]{:S(2)}, u32[]{:S(2)}) collective-permute-start(f32[64,1536]{1,0:T(8,128)S(1)} %get-tuple-element.532), channel_id=1, source_target_pairs={{4,0},{8,4},{12,8},{16,12},{20,16},{24,20},{28,24},{0,28},{5,1},{9... | collective-permute-start | bytes 1179656 | tf_op jit(solution)/shard_map/while/body/eval_jaxpr/ppermute | solution.py:12
Sparse Core Ops, SparseCore 0:
  54.7 50.8 all-reduce.1
Sparse Core Ops, SparseCore 1:
  58.3 28.1 reduce-scatter.1
where the time goes:
time: 146 us; the launch traced here: 145 us
  waiting for transfers between devices  73.3 us (50%)
  between operations  15.7 us (11%)
  other arithmetic  13.4 us (9%)
  local copies, waits for them, and re-layouts  12.1 us (8%)
  blocking collectives  11.6 us (8%)
  matrix products  9.87 us (7%)
  starting transfers between devices  8.66 us (6%)
    psum x1, waiting for transfers between devices, body(): weight_grad = lax.psum(grad_local, 'dom') * grad_scale  47.7 us
    ppermute x6, waiting for transfers between devices, shifted(): return lax.ppermute(block, axis, route)  25.5 us
    all_gather x1, blocking collectives, body(): slab_piece = lax.all_gather(hidden_t, 'feat', axis=0, tiled=True)  11.6 us
    ppermute x6, starting transfers between devices, shifted(): return lax.ppermute(block, axis, route)  8.58 us
    convert_element_type x8, other arithmetic, masked_table(): valid = (slots < used_slots).astype(jnp.float32)  5.2 us
    add x3, other arithmetic, retreat(): return shifted(running, 'dom', -1) + backward_piece(step_index)  3.48 us
    dot_general x4, matrix products, forward_piece(): jnp.einsum('fkc,krc->fkr', picked, values[step_index], preferred_element_...  3.02 us
  transfers between devices with their start and end apart: 8, of which 7 were waited for; matrix products, arithmetic and copies ran while one was open for 11% of the time, Pallas kernels for 0%

commit v1 on v0

v1 whole, which is shorter than its diff:
```python
import functools
import math

import jax
import jax.numpy as jnp
from jax import lax
from jax.experimental import pallas as pl
from jax.experimental.pallas import tpu as pltpu
from jax.sharding import PartitionSpec as P

MESH = pl.DeviceIdType.MESH
F32 = jnp.float32
BF16 = jnp.bfloat16
VMEM_LIMIT = 40 * 1024 * 1024


def lanes(index, side):
    return pl.ds(pl.multiple_of(index * side, side), side)


def pull_kernel(row_ref, col_ref, count_ref, cot_ref, val_ref, part_ref, own_ref, acc):
    s = pl.program_id(0)
    slots, side = val_ref.shape[1], val_ref.shape[3]
    nodes = cot_ref.shape[1]
    acc[...] = jnp.zeros_like(acc)
    count = count_ref[0, s]
    for k in range(slots):
        target = jnp.where(k < count, col_ref[0, s, k], nodes // side)
        term = jnp.dot(
            cot_ref[:, lanes(row_ref[0, s, k], side)],
            val_ref[0, k],
            preferred_element_type=F32,
        )
        acc[:, lanes(target, side)] += term
    total = acc[:, :nodes]
    part_ref[0] = total.astype(BF16)

    @pl.when(s == 0)
    def _():
        own_ref[...] = total


def push_kernel(row_ref, col_ref, count_ref, got_ref, val_ref, out_ref, acc):
    s = pl.program_id(0)
    slots, side = val_ref.shape[1], val_ref.shape[3]
    nodes = out_ref.shape[1]

    @pl.when(s == 0)
    def _():
        acc[...] = jnp.zeros_like(acc)

    count = count_ref[0, s]
    for k in range(slots):
        target = jnp.where(k < count, row_ref[0, s, k], nodes // side)
        term = lax.dot_general(
            got_ref[0, :, lanes(col_ref[0, s, k], side)],
            val_ref[0, k],
            (((1,), (1,)), ((), ())),
            preferred_element_type=F32,
        )
        acc[:, lanes(target, side)] += term

    @pl.when(s == pl.num_programs(0) - 1)
    def _():
        out_ref[...] = acc[:, :nodes].astype(BF16)


def exchange_kernel(
    n_dom, n_feat, scale,
    feat_ref, weight_ref, part_ref, own_ref,
    got_ref, wgrad_ref, fgrad_ref,
    all_feat, all_grad, w_rows, sib_part, sum_part, far_part, extra_part, pieces, wgrad_t,
    w_part, f_sem, w_sem, g_sem, sib_sem, far_sem, ex_sem, y_sem, yf_sem, ye_sem, rs_sem, ag_sem,
):
    steps, width, nodes = part_ref.shape
    pairs = steps // 2 - 1
    n_red = w_part.shape[0]
    me = lax.axis_index("dom")
    mine = lax.axis_index("feat")
    odd = lax.rem(me, 2)
    sib = me + 1 - 2 * odd
    extra = jnp.where(odd == 1, 1, steps - 1)
    y_extra = jnp.where(odd == 1, steps - 1, 1)

    def dom_at(offset):
        return lax.rem(me + offset + n_dom, n_dom)

    def feat_at(offset):
        return lax.rem(mine + offset + n_feat, n_feat)

    def to_dom(src, dst, sem, index, target):
        return pltpu.make_async_remote_copy(
            src_ref=src, dst_ref=dst, send_sem=sem.at[0, index], recv_sem=sem.at[1, index],
            device_id=(target, mine), device_id_type=MESH,
        )

    def to_feat(src, dst, sem, index, target):
        return pltpu.make_async_remote_copy(
            src_ref=src, dst_ref=dst, send_sem=sem.at[0, index], recv_sem=sem.at[1, index],
            device_id=(me, target), device_id_type=MESH,
        )

    barrier = pltpu.get_barrier_semaphore()

    def greet(k, carry):
        pl.semaphore_signal(barrier, inc=1, device_id=(dom_at(k), mine), device_id_type=MESH)
        return carry

    lax.fori_loop(1, n_dom, greet, 0)
    for k in range(1, n_feat):
        pl.semaphore_signal(barrier, inc=1, device_id=(me, feat_at(k)), device_id_type=MESH)
    pl.semaphore_wait(barrier, n_dom + n_feat - 2)

    my_rows = pl.ds(pl.multiple_of(mine * width, width), width)

    sib_copies = []
    for j in range(1, pairs + 1):
        c = to_dom(part_ref.at[2 * j - 1 + 2 * odd], sib_part.at[j - 1], sib_sem, j - 1, sib)
        c.start()
        sib_copies.append(c)
    f_copies, w_copies = [], []
    for k in range(1, n_feat):
        c = to_feat(feat_ref, all_feat.at[my_rows], f_sem, k - 1, feat_at(k))
        c.start()
        f_copies.append(c)
    ex_copy = to_dom(part_ref.at[extra], extra_part, ex_sem, 0, dom_at(-extra))
    ex_copy.start()
    for k in range(1, n_feat):
        there = feat_at(k)
        rows = pl.ds(pl.multiple_of(there * width, width), width)
        c = to_feat(weight_ref.at[rows], w_rows.at[mine], w_sem, k - 1, there)
        c.start()
        w_copies.append(c)
    far_copies = []
    for j in range(1, pairs + 1):
        sib_copies[j - 1].wait_recv()
        sum_part[j - 1] = (part_ref[2 * j].astype(F32) + sib_part[j - 1].astype(F32)).astype(BF16)
        c = to_dom(sum_part.at[j - 1], far_part.at[j - 1], far_sem, j - 1, dom_at(-2 * j))
        c.start()
        far_copies.append(c)
    all_feat[my_rows] = feat_ref[...]
    w_rows[mine] = weight_ref[my_rows]

    for c in f_copies:
        c.wait_recv()
    y = lax.dot_general(
        weight_ref[...], all_feat[...], (((0,), (0,)), ((), ())), preferred_element_type=F32
    )
    got_ref[0] = y.astype(BF16)
    y_copies = []
    for j in range(1, pairs + 1):
        c = to_dom(got_ref.at[0], got_ref.at[2 * j], y_sem, j - 1, dom_at(2 * j))
        c.start()
        y_copies.append(c)
    ye_copy = to_dom(got_ref.at[0], got_ref.at[y_extra], ye_sem, 0, dom_at(y_extra))
    ye_copy.start()

    total = own_ref[...]
    for j in range(1, pairs + 1):
        far_copies[j - 1].wait_recv()
        total += far_part[j - 1].astype(F32)
    ex_copy.wait_recv()
    total += extra_part[...].astype(F32)
    all_grad[my_rows] = total.astype(BF16)
    g_copies = []
    for k in range(1, n_feat):
        c = to_feat(all_grad.at[my_rows], all_grad.at[my_rows], g_sem, k - 1, feat_at(k))
        c.start()
        g_copies.append(c)
    w_term = lax.dot_general(
        all_grad[my_rows], all_feat[...], (((1,), (1,)), ((), ())), preferred_element_type=F32
    )
    for i in range(n_red):
        w_part[i] = w_term[8 * i:8 * i + 8]

    def when(cond, run):
        if cond is None:
            run()
        else:
            pl.when(cond)(run)

    def reducer(index):
        return None if n_red == n_dom else index < n_red

    def rs_copy(k):
        there = dom_at(k)
        piece = there if n_red == n_dom else lax.rem(there, n_red)
        return to_dom(w_part.at[piece], pieces.at[me], rs_sem, k - 1, there)

    def ag_copy(k):
        piece = me if n_red == n_dom else lax.rem(me, n_red)
        return to_dom(wgrad_t.at[piece], wgrad_t.at[piece], ag_sem, k - 1, dom_at(k))

    def each(make):
        def step(k, carry):
            make(k)
            return carry

        lax.fori_loop(1, n_dom, step, 0)

    each(lambda k: when(reducer(dom_at(k)), lambda: rs_copy(k).start()))

    yf_copies = []
    for j in range(1, pairs + 1):
        y_copies[j - 1].wait_recv()
        c = to_dom(got_ref.at[2 * j], got_ref.at[2 * j + 1 - 2 * odd], yf_sem, j - 1, sib)
        c.start()
        yf_copies.append(c)

    def reduce_piece():
        piece = me if n_red == n_dom else lax.rem(me, n_red)
        pieces[me] = w_part[piece]
        each(lambda k: rs_copy(k).wait_recv())
        wgrad_t[piece] = jnp.sum(pieces[...], axis=0) * scale
        each(lambda k: ag_copy(k).start())

    when(reducer(me), reduce_piece)

    for c in w_copies + g_copies:
        c.wait_recv()
    w_mine = jnp.concatenate([w_rows[k] for k in range(n_feat)], axis=1)
    fgrad_ref[...] = jnp.dot(w_mine, all_grad[...], preferred_element_type=F32).astype(BF16)

    each(lambda k: when(reducer(dom_at(-k)), lambda: ag_copy(k).wait_recv()))
    wgrad_ref[...] = wgrad_t[...].reshape(width, -1).T

    for c in yf_copies + [ye_copy]:
        c.wait_recv()
    for c in sib_copies + f_copies + w_copies + far_copies + [ex_copy] + y_copies + [ye_copy]:
        c.wait_send()
    for c in g_copies + yf_copies:
        c.wait_send()
    each(lambda k: when(reducer(dom_at(k)), lambda: rs_copy(k).wait_send()))
    when(reducer(me), lambda: each(lambda k: ag_copy(k).wait_send()))


def body(n_dom, n_feat, features_t, weight, tile_values, row_tiles, col_tiles, tile_counts, cotangent_t):
    width, nodes = features_t.shape
    hid = weight.shape[0]
    _, steps, slots, side, _ = tile_values.shape
    values = tile_values[0]
    smem = pl.BlockSpec(memory_space=pltpu.SMEM)
    vmem = pl.BlockSpec(memory_space=pltpu.VMEM)
    tile_spec = pl.BlockSpec((1, slots, side, side), lambda s: (s, 0, 0, 0))
    step_spec = pl.BlockSpec((1, width, nodes), lambda s: (s, 0, 0))
    full_spec = pl.BlockSpec((width, nodes), lambda s: (0, 0))
    acc = pltpu.VMEM((width, nodes + side), F32)

    part, own = pl.pallas_call(
        pull_kernel,
        grid=(steps,),
        out_shape=(
            jax.ShapeDtypeStruct((steps, width, nodes), BF16),
            jax.ShapeDtypeStruct((width, nodes), F32),
        ),
        in_specs=[smem, smem, smem, full_spec, tile_spec],
        out_specs=(step_spec, full_spec),
        scratch_shapes=[acc],
        compiler_params=pltpu.CompilerParams(vmem_limit_bytes=VMEM_LIMIT),
        name="pull",
    )(row_tiles, col_tiles, tile_counts, cotangent_t, values)

    pairs = steps // 2 - 1
    n_red = min(width // 8, n_dom)

    def sems(count):
        return pltpu.SemaphoreType.DMA((2, count))

    got, weight_grad, feature_grad_t = pl.pallas_call(
        functools.partial(exchange_kernel, n_dom, n_feat, 1.0 / math.sqrt(nodes * n_dom)),
        out_shape=(
            jax.ShapeDtypeStruct((steps, width, nodes), BF16),
            jax.ShapeDtypeStruct((hid, width), F32),
            jax.ShapeDtypeStruct((width, nodes), BF16),
        ),
        in_specs=[vmem] * 4,
        out_specs=(vmem,) * 3,
        scratch_shapes=[
            pltpu.VMEM((hid, nodes), BF16),
            pltpu.VMEM((hid, nodes), BF16),
            pltpu.VMEM((n_feat, width, width), BF16),
            pltpu.VMEM((pairs, width, nodes), BF16),
            pltpu.VMEM((pairs, width, nodes), BF16),
            pltpu.VMEM((pairs, width, nodes), BF16),
            pltpu.VMEM((width, nodes), BF16),
            pltpu.VMEM((n_dom, 8, hid), F32),
            pltpu.VMEM((n_red, 8, hid), F32),
            pltpu.VMEM((n_red, 8, hid), F32),
            sems(n_feat - 1), sems(n_feat - 1), sems(n_feat - 1),
            sems(pairs), sems(pairs), sems(1),
            sems(pairs), sems(pairs), sems(1),
            sems(n_dom - 1), sems(n_dom - 1),
        ],
        compiler_params=pltpu.CompilerParams(
            vmem_limit_bytes=VMEM_LIMIT, collective_id=0, has_side_effects=True
        ),
        name="exchange",
    )(features_t, weight, part, own)

    output_t = pl.pallas_call(
        push_kernel,
        grid=(steps,),
        out_shape=jax.ShapeDtypeStruct((width, nodes), BF16),
        in_specs=[smem, smem, smem, step_spec, tile_spec],
        out_specs=full_spec,
        scratch_shapes=[acc],
        compiler_params=pltpu.CompilerParams(vmem_limit_bytes=VMEM_LIMIT),
        name="push",
    )(row_tiles, col_tiles, tile_counts, got, values)
    return output_t, weight_grad, feature_grad_t


def solution(mesh):
    in_specs = (
        P("feat", "dom"),
        P(None, "feat"),
        P("dom", None, None, None, None),
        P("dom", None, None),
        P("dom", None, None),
        P("dom", None),
        P("feat", "dom"),
    )
    out_specs = (P("feat", "dom"), P(None, "feat"), P("feat", "dom"))
    local = functools.partial(body, mesh.shape["dom"], mesh.shape["feat"])
    return jax.shard_map(local, mesh=mesh, in_specs=in_specs, out_specs=out_specs, check_vma=False)
```

time: 146 us -> 45 us (0.31)
  waiting for transfers between devices: 73.3 us -> 0 us
  Pallas kernels: 0 us -> 37.2 us
  between operations: 15.7 us -> 0.68 us
  other arithmetic: 13.4 us -> 0 us
  blocking collectives: 11.6 us -> 0 us
  matrix products: 9.87 us -> 0 us
  starting transfers between devices: 8.66 us -> 0 us
  local copies, waits for them, and re-layouts: 12.1 us -> 6.8 us
    psum x1 -> x0, waiting for transfers between devices: 47.7 us -> none  [body(): weight_grad = lax.psum(grad_local, 'dom') * grad_scale]
    pallas_call x0 -> x3, Pallas kernels: none -> 37.2 us  [the longest x1 32 us: body(): pl.pallas_call(functools.partial(exchange_kernel, n_dom, n_feat, 1.0 / ma...]
    ppermute x6 -> x0, waiting for transfers between devices: 25.5 us -> none  [shifted(): return lax.ppermute(block, axis, route)]
    all_gather x1 -> x0, blocking collectives: 11.6 us -> none  [body(): slab_piece = lax.all_gather(hidden_t, 'feat', axis=0, tiled=True)]
    dot_general x19 -> x0, matrix products: 9.87 us -> none  [the longest x4 3.02 us: forward_piece(): jnp.einsum('fkc,krc->fkr', picked, values[step_index], preferred_element_...]
    ppermute x6 -> x0, starting transfers between devices: 8.58 us -> none  [shifted(): return lax.ppermute(block, axis, route)]
    convert_element_type x11 -> x0, other arithmetic: 5.95 us -> none  [the longest x8 5.2 us: masked_table(): valid = (slots < used_slots).astype(jnp.float32)]
    unnamed x17, local copies, waits for them, and re-layouts: 1.37 us -> 6.8 us
  transfers between devices with their start and end apart: 8 -> 0, of which waited for: 7 -> 0; matrix products, arithmetic and copies ran while one was open for 11% -> 0% of each run, Pallas kernels for 0% -> 0%
where the time goes in v1:
time: 45 us; the launch traced here: 44.7 us
  Pallas kernels  37.2 us (83%)
  local copies, waits for them, and re-layouts  6.8 us (15%)
  between operations  0.68 us (2%)
    pallas_call x1, Pallas kernels, body(): pl.pallas_call(functools.partial(exchange_kernel, n_dom, n_feat, 1.0 / ma...  32 us
    unnamed x17, local copies, waits for them, and re-layouts  6.8 us
    pallas_call x1, Pallas kernels, body(): pl.pallas_call(push_kernel, grid=(steps,), out_shape=jax.ShapeDtypeStruct...  3.28 us
    pallas_call x1, Pallas kernels, body(): pl.pallas_call(pull_kernel, grid=(steps,), out_shape=(jax.ShapeDtypeStruc...  1.95 us

profile of v1, /device:TPU:0, one launch (start us, length us, event | category | flops | bytes accessed | tf_op | source)
XLA Modules:
  0.0 44.7 jit_solution(13246868011618354947)
XLA Ops:
  0.6 0.9 %copy.10.weight_ref = bf16[256,64]{1,0:T(8,128)(2,1)S(1)} copy(bf16[256,64]{0,1:T(8,128)(2,1)} %param.8) | data formatting | bytes 65536 | tf_op args[1]
  1.5 0.0 copy-start
  1.5 1.6 %copy-done = bf16[1,4,16,128,128]{4,3,2,1,0:T(8,128)(2,1)S(1)} copy-done((bf16[1,4,16,128,128]{4,3,2,1,0:T(8,128)(2,1)S(1)}, bf16[1,4,16,128,128]{4,3,2,1,0:T(8,128)(2,1)}, u32[]{:S(2)}) %copy-start) | copy-done | bytes 2097176
  3.1 0.0 copy-start.2
  3.1 0.9 %copy-done.2 = bf16[64,1536]{1,0:T(8,128)(2,1)S(1)} copy-done((bf16[64,1536]{1,0:T(8,128)(2,1)S(1)}, bf16[64,1536]{1,0:T(8,128)(2,1)}, u32[]{:S(2)}) %copy-start.2) | copy-done | bytes 196632
  4.0 0.0 copy-start.4
  4.0 0.7 %copy-done.4 = s32[1,4,16]{2,1,0:T(4,128)S(1)} copy-done((s32[1,4,16]{2,1,0:T(4,128)S(1)}, s32[1,4,16]{2,1,0:T(4,128)}, u32[]{:S(2)}) %copy-start.4) | copy-done | bytes 280
  4.7 0.0 copy-start.5
  4.7 0.7 %copy-done.5 = s32[1,4,16]{2,1,0:T(4,128)S(1)} copy-done((s32[1,4,16]{2,1,0:T(4,128)S(1)}, s32[1,4,16]{2,1,0:T(4,128)}, u32[]{:S(2)}) %copy-start.5) | copy-done | bytes 280
  5.4 0.0 copy-start.6
  5.4 0.7 %copy-done.6 = s32[1,4]{1,0:T(1,128)S(1)} copy-done((s32[1,4]{1,0:T(1,128)S(1)}, s32[1,4]{1,0:T(1,128)}, u32[]{:S(2)}) %copy-start.6) | copy-done | bytes 40
  6.0 0.0 copy-start.3
  6.1 0.0 copy-start.1
  6.1 2.0 %pull.1 = (bf16[4,64,1536]{2,1,0:T(8,128)(2,1)S(1)}, f32[64,1536]{1,0:T(8,128)S(1)}) custom-call(s32[1,4,16]{2,1,0:T(4,128)S(1)} %copy-done.4, s32[1,4,16]{2,1,0:T(4,128)S(1)} %copy-done.5, s32[1,4]{1,0:T(1,128)S(1)} %copy-done.6, bf16[64,1536]{1,0:T(8,128)(2,1)S(1)} %copy-done.2, bf16[4,16,128,128]{3,2,1,0:T(8,128)(2,1)S(1)} %bitcast.1), custom_call_target="tpu_custom_call" | custom-call | tf_op jit(solution)/shard_map/pull/pallas_call | solution.py:249
  8.0 0.0 copy-done.3
  8.0 32.0 %exchange.1 = (bf16[4,64,1536]{2,1,0:T(8,128)(2,1)S(1)}, f32[256,64]{1,0:T(8,128)S(1)}, bf16[64,1536]{1,0:T(8,128)(2,1)S(1)}) custom-call(bf16[64,1536]{1,0:T(8,128)(2,1)S(1)} %copy-done.3, bf16[256,64]{1,0:T(8,128)(2,1)S(1)} %copy.10.weight_ref, bf16[4,64,1536]{2,1,0:T(8,128)(2,1)S(1)} %get-tuple-element.8.part_ref, f32[64,1536]{1,0:T(8,128)S(1)} %get-tuple-element.9.own_ref), custom_call_target="tpu_custom_call" | custom-call | tf_op jit(solution)/shard_map/exchange/pallas_call | solution.py:269
  40.0 0.0 copy-done.1
  40.0 3.3 %push.1 = bf16[64,1536]{1,0:T(8,128)(2,1)} custom-call(s32[1,4,16]{2,1,0:T(4,128)S(1)} %copy-done.4, s32[1,4,16]{2,1,0:T(4,128)S(1)} %copy-done.5, s32[1,4]{1,0:T(1,128)S(1)} %copy-done.6, bf16[4,64,1536]{2,1,0:T(8,128)(2,1)S(1)} %get-tuple-element.10.got_ref, bf16[4,16,128,128]{3,2,1,0:T(8,128)(2,1)S(1)} %bitcast.2), custom_call_target="tpu_custom_call" | custom-call | tf_op jit(solution)/shard_map/push/pallas_call | solution.py:300
  43.3 0.7 %copy.11 = f32[256,64]{0,1:T(8,128)} copy(f32[256,64]{1,0:T(8,128)S(1)} %get-tuple-element.14) | data formatting | bytes 131072
  44.0 0.7 %copy.13 = bf16[64,1536]{1,0:T(8,128)(2,1)} copy(bf16[64,1536]{1,0:T(8,128)(2,1)S(1)} %get-tuple-element.21) | data formatting | bytes 393216
Async XLA Ops:
  1.5 1.6 %copy-start = (bf16[1,4,16,128,128]{4,3,2,1,0:T(8,128)(2,1)S(1)}, bf16[1,4,16,128,128]{4,3,2,1,0:T(8,128)(2,1)}, u32[]{:S(2)}) copy-start(bf16[1,4,16,128,128]{4,3,2,1,0:T(8,128)(2,1)} %param.9) | copy-start | bytes 6291460
  3.1 0.9 %copy-start.2 = (bf16[64,1536]{1,0:T(8,128)(2,1)S(1)}, bf16[64,1536]{1,0:T(8,128)(2,1)}, u32[]{:S(2)}) copy-start(bf16[64,1536]{1,0:T(8,128)(2,1)} %cot_ref.1) | copy-start | bytes 589828
  4.0 0.7 %copy-start.4 = (s32[1,4,16]{2,1,0:T(4,128)S(1)}, s32[1,4,16]{2,1,0:T(4,128)}, u32[]{:S(2)}) copy-start(s32[1,4,16]{2,1,0:T(4,128)} %row_ref.3) | copy-start | bytes 772
  4.7 0.7 %copy-start.5 = (s32[1,4,16]{2,1,0:T(4,128)S(1)}, s32[1,4,16]{2,1,0:T(4,128)}, u32[]{:S(2)}) copy-start(s32[1,4,16]{2,1,0:T(4,128)} %col_ref.3) | copy-start | bytes 772
  5.4 0.7 %copy-start.6 = (s32[1,4]{1,0:T(1,128)S(1)}, s32[1,4]{1,0:T(1,128)}, u32[]{:S(2)}) copy-start(s32[1,4]{1,0:T(1,128)} %count_ref.3) | copy-start | bytes 52
  6.0 2.0 %copy-start.3 = (bf16[64,1536]{1,0:T(8,128)(2,1)S(1)}, bf16[64,1536]{1,0:T(8,128)(2,1)}, u32[]{:S(2)}) copy-start(bf16[64,1536]{1,0:T(8,128)(2,1)} %feat_ref.1) | copy-start | bytes 589828
  6.1 34.0 %copy-start.1 = (bf16[1,4,16,128,128]{4,3,2,1,0:T(8,128)(2,1)S(1)}, bf16[1,4,16,128,128]{4,3,2,1,0:T(8,128)(2,1)}, u32[]{:S(2)}) copy-start(bf16[1,4,16,128,128]{4,3,2,1,0:T(8,128)(2,1)} %param.9) | copy-start | bytes 6291460

commit v2 on v1

v2 whole, which is shorter than its diff:
```python
import functools
import math

import jax
import jax.numpy as jnp
from jax import lax
from jax.experimental import pallas as pl
from jax.experimental.pallas import tpu as pltpu
from jax.sharding import PartitionSpec as P

MESH = pl.DeviceIdType.MESH
F32 = jnp.float32
BF16 = jnp.bfloat16
VMEM_LIMIT = 40 * 1024 * 1024


def lanes(index, side):
    return pl.ds(pl.multiple_of(index * side, side), side)


def pull_kernel(
    row_hbm, col_hbm, count_hbm, cot_hbm, val_hbm, part_ref, own_ref,
    row_ref, col_ref, count_ref, cot_ref, val_ref, acc, sem, val_sem,
):
    steps, slots, side = val_ref.shape[0], val_ref.shape[1], val_ref.shape[3]
    nodes = cot_ref.shape[1]
    small = [
        pltpu.make_async_copy(src, dst, sem.at[i])
        for i, (src, dst) in enumerate(
            [(row_hbm, row_ref), (col_hbm, col_ref), (count_hbm, count_ref), (cot_hbm, cot_ref)]
        )
    ]
    for c in small:
        c.start()

    def val_copy(s):
        return pltpu.make_async_copy(val_hbm.at[s], val_ref.at[s], val_sem.at[s])

    for s in range(steps):
        val_copy(s).start()
    for c in small:
        c.wait()

    def one(s, carry):
        acc[...] = jnp.zeros_like(acc)
        count = count_ref[0, s]
        val_copy(s).wait()
        for k in range(slots):
            target = jnp.where(k < count, col_ref[0, s, k], nodes // side)
            term = jnp.dot(
                cot_ref[:, lanes(row_ref[0, s, k], side)],
                val_ref[s, k],
                preferred_element_type=F32,
            )
            acc[:, lanes(target, side)] += term
        total = acc[:, :nodes]
        part_ref[s] = total.astype(BF16)

        @pl.when(s == 0)
        def _():
            own_ref[...] = total

        return carry

    lax.fori_loop(0, steps, one, 0)


def push_kernel(row_ref, col_ref, count_ref, got_ref, val_ref, out_ref, acc):
    steps, slots, side = val_ref.shape[0], val_ref.shape[1], val_ref.shape[3]
    nodes = out_ref.shape[1]
    acc[...] = jnp.zeros_like(acc)

    def one(s, carry):
        count = count_ref[0, s]
        for k in range(slots):
            target = jnp.where(k < count, row_ref[0, s, k], nodes // side)
            term = lax.dot_general(
                got_ref[s, :, lanes(col_ref[0, s, k], side)],
                val_ref[s, k],
                (((1,), (1,)), ((), ())),
                preferred_element_type=F32,
            )
            acc[:, lanes(target, side)] += term
        return carry

    lax.fori_loop(0, steps, one, 0)
    out_ref[...] = acc[:, :nodes].astype(BF16)


def exchange_kernel(
    n_dom, n_feat, scale,
    feat_ref, weight_ref, part_ref, own_ref,
    got_ref, wgrad_ref, fgrad_ref,
    all_feat, all_grad, w_cols, sib_part, sum_part, far_part, extra_part, pieces, wgrad_t,
    w_part, w_out, f_sem, w_sem, g_sem, sib_sem, far_sem, ex_sem, y_sem, yf_sem, ye_sem, rs_sem, ag_sem,
):
    steps, width, nodes = part_ref.shape
    pairs = steps // 2 - 1
    n_red = w_part.shape[0]
    me = lax.axis_index("dom")
    mine = lax.axis_index("feat")
    odd = lax.rem(me, 2)
    sib = me + 1 - 2 * odd
    extra = jnp.where(odd == 1, 1, steps - 1)
    y_extra = jnp.where(odd == 1, steps - 1, 1)

    def dom_at(offset):
        return lax.rem(me + offset + n_dom, n_dom)

    def feat_at(offset):
        return lax.rem(mine + offset + n_feat, n_feat)

    def to_dom(src, dst, sem, index, target):
        return pltpu.make_async_remote_copy(
            src_ref=src, dst_ref=dst, send_sem=sem.at[0, index], recv_sem=sem.at[1, index],
            device_id=(target, mine), device_id_type=MESH,
        )

    def to_feat(src, dst, sem, index, target):
        return pltpu.make_async_remote_copy(
            src_ref=src, dst_ref=dst, send_sem=sem.at[0, index], recv_sem=sem.at[1, index],
            device_id=(me, target), device_id_type=MESH,
        )

    barrier = pltpu.get_barrier_semaphore()

    def greet(k, carry):
        pl.semaphore_signal(barrier, inc=1, device_id=(dom_at(k), mine), device_id_type=MESH)
        return carry

    lax.fori_loop(1, n_dom, greet, 0)
    for k in range(1, n_feat):
        pl.semaphore_signal(barrier, inc=1, device_id=(me, feat_at(k)), device_id_type=MESH)
    pl.semaphore_wait(barrier, n_dom + n_feat - 2)

    half = width // 2
    group = n_feat // 2
    high = feat_at(group)
    base = lax.div(mine, group) * group

    def low(offset):
        return base + lax.rem(mine - base + offset + group, group)

    def gather(buf, sem):
        def copy(block, part, index, target):
            rows = buf.at[pl.ds(pl.multiple_of(block * width + part * half, half), half)]
            return to_feat(rows, rows, sem, index, target)

        near = [
            [copy(mine, h, 2 * (k - 1) + h, low(k)) for h in range(2)] for k in range(1, group)
        ]
        across = [copy(mine, h, 2 * (group - 1) + h, high) for h in range(2)]
        pass_high = [copy(low(-k), 0, 2 * group + k - 1, high) for k in range(1, group)]
        pass_near = [copy(high, 1, 3 * group + k - 2, low(k)) for k in range(1, group)]
        every = [c for two in near for c in two] + across + pass_high + pass_near

        def begin():
            for k in range(group - 1):
                near[k][0].start()
            across[1].start()
            for k in range(group - 1):
                near[k][1].start()
            across[0].start()

        def forward():
            for k in range(group - 1):
                near[k][0].wait_recv()
                pass_high[k].start()
            across[1].wait_recv()
            for c in pass_near:
                c.start()

        def arrive():
            for k in range(group - 1):
                near[k][1].wait_recv()
            across[0].wait_recv()
            for c in pass_high + pass_near:
                c.wait_recv()

        def sent():
            for c in every:
                c.wait_send()

        return begin, forward, arrive, sent

    my_rows = pl.ds(pl.multiple_of(mine * width, width), width)

    sib_copies = []
    for j in range(1, pairs + 1):
        c = to_dom(part_ref.at[2 * j - 1 + 2 * odd], sib_part.at[j - 1], sib_sem, j - 1, sib)
        c.start()
        sib_copies.append(c)
    all_feat[my_rows] = feat_ref[...]
    f_begin, f_forward, f_arrive, f_sent = gather(all_feat, f_sem)
    g_begin, g_forward, g_arrive, g_sent = gather(all_grad, g_sem)
    f_begin()
    far_copies = []
    for j in range(1, pairs + 1):
        sib_copies[j - 1].wait_recv()
        sum_part[j - 1] = (part_ref[2 * j].astype(F32) + sib_part[j - 1].astype(F32)).astype(BF16)
        c = to_dom(sum_part.at[j - 1], far_part.at[j - 1], far_sem, j - 1, dom_at(-2 * j))
        c.start()
        far_copies.append(c)
    ex_copy = to_dom(part_ref.at[extra], extra_part, ex_sem, 0, dom_at(-extra))
    ex_copy.start()
    weight = weight_ref[...].T
    for k in range(n_feat):
        w_out[k] = weight[k * width:(k + 1) * width]
    w_copies = []
    for k in range(1, n_feat):
        c = to_feat(w_out.at[feat_at(k)], w_cols.at[mine], w_sem, k - 1, feat_at(k))
        c.start()
        w_copies.append(c)
    w_cols[mine] = w_out[mine]
    f_forward()

    total = own_ref[...]
    for j in range(1, pairs + 1):
        far_copies[j - 1].wait_recv()
        total += far_part[j - 1].astype(F32)
    ex_copy.wait_recv()
    total += extra_part[...].astype(F32)
    all_grad[my_rows] = total.astype(BF16)
    f_arrive()
    g_begin()

    y = jnp.dot(weight_ref[...], all_feat[...], preferred_element_type=F32)
    got_ref[0] = y.astype(BF16)
    y_copies = []
    for j in range(1, pairs + 1):
        c = to_dom(got_ref.at[0], got_ref.at[2 * j], y_sem, j - 1, dom_at(2 * j))
        c.start()
        y_copies.append(c)

    w_term = lax.dot_general(
        all_grad[my_rows], all_feat[...], (((1,), (1,)), ((), ())), preferred_element_type=F32
    )
    for i in range(n_red):
        w_part[i] = w_term[8 * i:8 * i + 8]

    def when(cond, run):
        if cond is None:
            run()
        else:
            pl.when(cond)(run)

    def reducer(index):
        return None if n_red == n_dom else index < n_red

    my_piece = me if n_red == n_dom else lax.rem(me, n_red)

    def rs_copy(k):
        there = dom_at(k)
        piece = there if n_red == n_dom else lax.rem(there, n_red)
        return to_dom(w_part.at[piece], pieces.at[me], rs_sem, k - 1, there)

    def ag_copy(k):
        return to_dom(wgrad_t.at[my_piece], wgrad_t.at[my_piece], ag_sem, k - 1, dom_at(k))

    def each(make):
        def step(k, carry):
            make(k)
            return carry

        lax.fori_loop(1, n_dom, step, 0)

    each(lambda k: when(reducer(dom_at(k)), lambda: rs_copy(k).start()))
    ye_copy = to_dom(got_ref.at[0], got_ref.at[y_extra], ye_sem, 0, dom_at(y_extra))
    ye_copy.start()
    g_forward()

    def reduce_piece():
        pieces[me] = w_part[my_piece]
        each(lambda k: rs_copy(k).wait_recv())
        wgrad_t[my_piece] = jnp.sum(pieces[...], axis=0) * scale
        each(lambda k: ag_copy(k).start())

    when(reducer(me), reduce_piece)

    yf_copies = []
    for j in range(1, pairs + 1):
        y_copies[j - 1].wait_recv()
        c = to_dom(got_ref.at[2 * j], got_ref.at[2 * j + 1 - 2 * odd], yf_sem, j - 1, sib)
        c.start()
        yf_copies.append(c)

    for c in w_copies:
        c.wait_recv()
    w_mine = jnp.concatenate([w_cols[k] for k in range(n_feat)], axis=1)
    g_arrive()
    fgrad_ref[...] = jnp.dot(w_mine, all_grad[...], preferred_element_type=F32).astype(BF16)

    each(lambda k: when(reducer(dom_at(-k)), lambda: ag_copy(k).wait_recv()))
    wgrad_ref[...] = wgrad_t[...].reshape(wgrad_ref.shape)

    for c in yf_copies + [ye_copy]:
        c.wait_recv()
    for c in sib_copies + w_copies + far_copies + [ex_copy] + y_copies + [ye_copy] + yf_copies:
        c.wait_send()
    f_sent()
    g_sent()
    each(lambda k: when(reducer(dom_at(k)), lambda: rs_copy(k).wait_send()))
    when(reducer(me), lambda: each(lambda k: ag_copy(k).wait_send()))


def body(n_dom, n_feat, features_t, weight, tile_values, row_tiles, col_tiles, tile_counts, cotangent_t):
    width, nodes = features_t.shape
    hid = weight.shape[0]
    _, steps, slots, side, _ = tile_values.shape
    values = tile_values[0]
    smem = pl.BlockSpec(memory_space=pltpu.SMEM)
    vmem = pl.BlockSpec(memory_space=pltpu.VMEM)
    hbm = pl.BlockSpec(memory_space=pltpu.HBM)
    acc = pltpu.VMEM((width, nodes + side), F32)

    part, own = pl.pallas_call(
        pull_kernel,
        out_shape=(
            jax.ShapeDtypeStruct((steps, width, nodes), BF16),
            jax.ShapeDtypeStruct((width, nodes), F32),
        ),
        in_specs=[hbm] * 5,
        out_specs=(vmem, vmem),
        scratch_shapes=[
            pltpu.SMEM(row_tiles.shape, jnp.int32),
            pltpu.SMEM(col_tiles.shape, jnp.int32),
            pltpu.SMEM(tile_counts.shape, jnp.int32),
            pltpu.VMEM((width, nodes), BF16),
            pltpu.VMEM(values.shape, BF16),
            acc,
            pltpu.SemaphoreType.DMA((4,)),
            pltpu.SemaphoreType.DMA((steps,)),
        ],
        compiler_params=pltpu.CompilerParams(vmem_limit_bytes=VMEM_LIMIT),
        name="pull",
    )(row_tiles, col_tiles, tile_counts, cotangent_t, values)

    pairs = steps // 2 - 1
    n_red = min(width // 8, n_dom)

    def sems(count):
        return pltpu.SemaphoreType.DMA((2, count))

    got, weight_grad, feature_grad_t = pl.pallas_call(
        functools.partial(exchange_kernel, n_dom, n_feat, 1.0 / math.sqrt(nodes * n_dom)),
        out_shape=(
            jax.ShapeDtypeStruct((steps, width, nodes), BF16),
            jax.ShapeDtypeStruct((width, hid), F32),
            jax.ShapeDtypeStruct((width, nodes), BF16),
        ),
        in_specs=[vmem] * 4,
        out_specs=(vmem,) * 3,
        scratch_shapes=[
            pltpu.VMEM((hid, nodes), BF16),
            pltpu.VMEM((hid, nodes), BF16),
            pltpu.VMEM((n_feat, width, width), BF16),
            pltpu.VMEM((pairs, width, nodes), BF16),
            pltpu.VMEM((pairs, width, nodes), BF16),
            pltpu.VMEM((pairs, width, nodes), BF16),
            pltpu.VMEM((width, nodes), BF16),
            pltpu.VMEM((n_dom, 8, hid), F32),
            pltpu.VMEM((n_red, 8, hid), F32),
            pltpu.VMEM((n_red, 8, hid), F32),
            pltpu.VMEM((n_feat, width, width), BF16),
            sems(2 * n_feat - 2), sems(n_feat - 1), sems(2 * n_feat - 2),
            sems(pairs), sems(pairs), sems(1),
            sems(pairs), sems(pairs), sems(1),
            sems(n_dom - 1), sems(n_dom - 1),
        ],
        compiler_params=pltpu.CompilerParams(
            vmem_limit_bytes=VMEM_LIMIT, collective_id=0, has_side_effects=True
        ),
        name="exchange",
    )(features_t, weight.T, part, own)

    output_t = pl.pallas_call(
        push_kernel,
        out_shape=jax.ShapeDtypeStruct((width, nodes), BF16),
        in_specs=[smem, smem, smem, vmem, vmem],
        out_specs=vmem,
        scratch_shapes=[acc],
        compiler_params=pltpu.CompilerParams(vmem_limit_bytes=VMEM_LIMIT),
        name="push",
    )(row_tiles, col_tiles, tile_counts, got, values)
    return output_t, weight_grad.T, feature_grad_t


def solution(mesh):
    in_specs = (
        P("feat", "dom"),
        P(None, "feat"),
        P("dom", None, None, None, None),
        P("dom", None, None),
        P("dom", None, None),
        P("dom", None),
        P("feat", "dom"),
    )
    out_specs = (P("feat", "dom"), P(None, "feat"), P("feat", "dom"))
    local = functools.partial(body, mesh.shape["dom"], mesh.shape["feat"])
    return jax.shard_map(local, mesh=mesh, in_specs=in_specs, out_specs=out_specs, check_vma=False)
```

time: 45 us -> 42.2 us (0.938)
  Pallas kernels: 37.2 us -> 34.6 us
    pallas_call x1, Pallas kernels: 32 us -> 29.3 us  [body(): pl.pallas_call(functools.partial(exchange_kernel, n_dom, n_feat, 1.0 / ma...]
    unnamed x17 -> x18, local copies, waits for them, and re-layouts: 6.8 us -> 6.59 us
where the time goes in v2:
time: 42.2 us; the launch traced here: 41.9 us
  Pallas kernels  34.6 us (82%)
  local copies, waits for them, and re-layouts  6.59 us (16%)
  between operations  0.69 us (2%)
    pallas_call x1, Pallas kernels, body(): pl.pallas_call(functools.partial(exchange_kernel, n_dom, n_feat, 1.0 / ma...  29.3 us
    unnamed x18, local copies, waits for them, and re-layouts  6.59 us
    pallas_call x1, Pallas kernels, body(): pl.pallas_call(push_kernel, out_shape=jax.ShapeDtypeStruct((width, nodes)...  3.19 us
    pallas_call x1, Pallas kernels, body(): pl.pallas_call(pull_kernel, out_shape=(jax.ShapeDtypeStruct((steps, width...  2.06 us

profile of v2, /device:TPU:0, one launch (start us, length us, event | category | flops | bytes accessed | tf_op | source)
XLA Modules:
  0.0 41.9 jit_solution(14900156397550728758)
XLA Ops:
  0.6 0.0 copy-start
  0.6 1.6 %copy-done = bf16[1,4,16,128,128]{4,3,2,1,0:T(8,128)(2,1)S(1)} copy-done((bf16[1,4,16,128,128]{4,3,2,1,0:T(8,128)(2,1)S(1)}, bf16[1,4,16,128,128]{4,3,2,1,0:T(8,128)(2,1)}, u32[]{:S(2)}) %copy-start) | copy-done | bytes 2097176
  2.2 0.0 copy-start.2
  2.2 0.9 %copy-done.2 = bf16[64,1536]{1,0:T(8,128)(2,1)S(1)} copy-done((bf16[64,1536]{1,0:T(8,128)(2,1)S(1)}, bf16[64,1536]{1,0:T(8,128)(2,1)}, u32[]{:S(2)}) %copy-start.2) | copy-done | bytes 196632
  3.2 0.0 copy-start.5
  3.2 0.7 %copy-done.5 = s32[1,4,16]{2,1,0:T(4,128)S(1)} copy-done((s32[1,4,16]{2,1,0:T(4,128)S(1)}, s32[1,4,16]{2,1,0:T(4,128)}, u32[]{:S(2)}) %copy-start.5) | copy-done | bytes 280
  3.8 0.0 copy-start.6
  3.8 0.7 %copy-done.6 = s32[1,4,16]{2,1,0:T(4,128)S(1)} copy-done((s32[1,4,16]{2,1,0:T(4,128)S(1)}, s32[1,4,16]{2,1,0:T(4,128)}, u32[]{:S(2)}) %copy-start.6) | copy-done | bytes 280
  4.5 0.0 copy-start.7
  4.5 0.7 %copy-done.7 = s32[1,4]{1,0:T(1,128)S(1)} copy-done((s32[1,4]{1,0:T(1,128)S(1)}, s32[1,4]{1,0:T(1,128)}, u32[]{:S(2)}) %copy-start.7) | copy-done | bytes 40
  5.2 0.0 copy-start.3
  5.2 0.0 copy-start.1
  5.2 2.1 %pull.1 = (bf16[4,64,1536]{2,1,0:T(8,128)(2,1)S(1)}, f32[64,1536]{1,0:T(8,128)S(1)}) custom-call(s32[1,4,16]{2,1,0:T(4,128)S(1)} %copy-done.5, s32[1,4,16]{2,1,0:T(4,128)S(1)} %copy-done.6, s32[1,4]{1,0:T(1,128)S(1)} %copy-done.7, bf16[64,1536]{1,0:T(8,128)(2,1)S(1)} %copy-done.2, bf16[4,16,128,128]{3,2,1,0:T(8,128)(2,1)S(1)} %bitcast.3), custom_call_target="tpu_custom_call" | custom-call | tf_op jit(solution)/shard_map/pull/pallas_call | solution.py:316
  7.2 0.0 copy-done.3
  7.3 0.0 copy-start.4
  7.3 0.7 %copy-done.4 = bf16[256,64]{0,1:T(8,128)(2,1)S(1)} copy-done((bf16[256,64]{0,1:T(8,128)(2,1)S(1)}, bf16[256,64]{0,1:T(8,128)(2,1)}, u32[]{:S(2)}) %copy-start.4) | copy-done | bytes 32792
  8.0 29.3 %exchange.1 = (bf16[4,64,1536]{2,1,0:T(8,128)(2,1)S(1)}, f32[64,256]{1,0:T(8,128)S(1)}, bf16[64,1536]{1,0:T(8,128)(2,1)S(1)}) custom-call(bf16[64,1536]{1,0:T(8,128)(2,1)S(1)} %copy-done.3, bf16[64,256]{1,0:T(8,128)(2,1)S(1)} %bitcast.6, bf16[4,64,1536]{2,1,0:T(8,128)(2,1)S(1)} %get-tuple-element.8.part_ref, f32[64,1536]{1,0:T(8,128)S(1)} %get-tuple-element.9.own_ref), custom_call_target="tpu_custom_call" | custom-call | tf_op jit(solution)/shard_map/exchange/pallas_call | solution.py:344
  37.4 0.0 copy-done.1
  37.4 3.2 %push.1 = bf16[64,1536]{1,0:T(8,128)(2,1)} custom-call(s32[1,4,16]{2,1,0:T(4,128)S(1)} %copy-done.5, s32[1,4,16]{2,1,0:T(4,128)S(1)} %copy-done.6, s32[1,4]{1,0:T(1,128)S(1)} %copy-done.7, bf16[4,64,1536]{2,1,0:T(8,128)(2,1)S(1)} %get-tuple-element.10.got_ref, bf16[4,16,128,128]{3,2,1,0:T(8,128)(2,1)S(1)} %bitcast.4), custom_call_target="tpu_custom_call" | custom-call | tf_op jit(solution)/shard_map/push/pallas_call | solution.py:376
  40.6 0.6 %copy.12 = f32[256,64]{0,1:T(8,128)} copy(f32[256,64]{0,1:T(8,128)S(1)} %bitcast.5) | data formatting | bytes 131072
  41.2 0.7 %copy.13 = bf16[64,1536]{1,0:T(8,128)(2,1)} copy(bf16[64,1536]{1,0:T(8,128)(2,1)S(1)} %get-tuple-element.18) | data formatting | bytes 393216
Async XLA Ops:
  0.6 1.6 %copy-start = (bf16[1,4,16,128,128]{4,3,2,1,0:T(8,128)(2,1)S(1)}, bf16[1,4,16,128,128]{4,3,2,1,0:T(8,128)(2,1)}, u32[]{:S(2)}) copy-start(bf16[1,4,16,128,128]{4,3,2,1,0:T(8,128)(2,1)} %param.9) | copy-start | bytes 6291460
  2.2 0.9 %copy-start.2 = (bf16[64,1536]{1,0:T(8,128)(2,1)S(1)}, bf16[64,1536]{1,0:T(8,128)(2,1)}, u32[]{:S(2)}) copy-start(bf16[64,1536]{1,0:T(8,128)(2,1)} %cot_hbm.1) | copy-start | bytes 589828
  3.2 0.7 %copy-start.5 = (s32[1,4,16]{2,1,0:T(4,128)S(1)}, s32[1,4,16]{2,1,0:T(4,128)}, u32[]{:S(2)}) copy-start(s32[1,4,16]{2,1,0:T(4,128)} %row_ref.1) | copy-start | bytes 772
  3.8 0.7 %copy-start.6 = (s32[1,4,16]{2,1,0:T(4,128)S(1)}, s32[1,4,16]{2,1,0:T(4,128)}, u32[]{:S(2)}) copy-start(s32[1,4,16]{2,1,0:T(4,128)} %col_ref.1) | copy-start | bytes 772
  4.5 0.7 %copy-start.7 = (s32[1,4]{1,0:T(1,128)S(1)}, s32[1,4]{1,0:T(1,128)}, u32[]{:S(2)}) copy-start(s32[1,4]{1,0:T(1,128)} %count_ref.1) | copy-start | bytes 52
  5.2 2.1 %copy-start.3 = (bf16[64,1536]{1,0:T(8,128)(2,1)S(1)}, bf16[64,1536]{1,0:T(8,128)(2,1)}, u32[]{:S(2)}) copy-start(bf16[64,1536]{1,0:T(8,128)(2,1)} %feat_ref.1) | copy-start | bytes 589828
  5.2 32.2 %copy-start.1 = (bf16[1,4,16,128,128]{4,3,2,1,0:T(8,128)(2,1)S(1)}, bf16[1,4,16,128,128]{4,3,2,1,0:T(8,128)(2,1)}, u32[]{:S(2)}) copy-start(bf16[1,4,16,128,128]{4,3,2,1,0:T(8,128)(2,1)} %param.9) | copy-start | bytes 6291460
  7.3 0.8 %copy-start.4 = (bf16[256,64]{0,1:T(8,128)(2,1)S(1)}, bf16[256,64]{0,1:T(8,128)(2,1)}, u32[]{:S(2)}) copy-start(bf16[256,64]{0,1:T(8,128)(2,1)} %param.8) | copy-start | bytes 98308

commit v3 on v2

--- a/solution.py
+++ b/solution.py
@@ -12,6 +12,9 @@
 F32 = jnp.float32
 BF16 = jnp.bfloat16
 VMEM_LIMIT = 40 * 1024 * 1024
+PULL_LIMIT = 62 * 1024 * 1024
+CUTS = 3
+PIECE = 16
 
 
 def lanes(index, side):
@@ -190,6 +193,8 @@
         c = to_dom(part_ref.at[2 * j - 1 + 2 * odd], sib_part.at[j - 1], sib_sem, j - 1, sib)
         c.start()
         sib_copies.append(c)
+    ex_copy = to_dom(part_ref.at[extra], extra_part, ex_sem, 0, dom_at(-extra))
+    ex_copy.start()
     all_feat[my_rows] = feat_ref[...]
     f_begin, f_forward, f_arrive, f_sent = gather(all_feat, f_sem)
     g_begin, g_forward, g_arrive, g_sent = gather(all_grad, g_sem)
@@ -201,8 +206,6 @@
         c = to_dom(sum_part.at[j - 1], far_part.at[j - 1], far_sem, j - 1, dom_at(-2 * j))
         c.start()
         far_copies.append(c)
-    ex_copy = to_dom(part_ref.at[extra], extra_part, ex_sem, 0, dom_at(-extra))
-    ex_copy.start()
     weight = weight_ref[...].T
     for k in range(n_feat):
         w_out[k] = weight[k * width:(k + 1) * width]
@@ -214,29 +217,37 @@
     w_cols[mine] = w_out[mine]
     f_forward()
 
+    cut = nodes // CUTS
+    y_copies = [[] for _ in range(pairs)]
+    ye_copies = []
+    f_arrive()
+    for i in range(CUTS):
+        cols = pl.ds(i * cut, cut)
+        y = jnp.dot(weight_ref[...], all_feat[:, cols], preferred_element_type=F32)
+        got_ref[0, :, cols] = y.astype(BF16)
+        here = got_ref.at[0, :, cols]
+        c = to_dom(here, got_ref.at[y_extra, :, cols], ye_sem, i, dom_at(y_extra))
+        c.start()
+        ye_copies.append(c)
+        for j in range(1, pairs + 1):
+            c = to_dom(here, got_ref.at[2 * j, :, cols], y_sem, (j - 1) * CUTS + i, dom_at(2 * j))
+            c.start()
+            y_copies[j - 1].append(c)
+
     total = own_ref[...]
+    ex_copy.wait_recv()
+    total += extra_part[...].astype(F32)
     for j in range(1, pairs + 1):
         far_copies[j - 1].wait_recv()
         total += far_part[j - 1].astype(F32)
-    ex_copy.wait_recv()
-    total += extra_part[...].astype(F32)
     all_grad[my_rows] = total.astype(BF16)
-    f_arrive()
     g_begin()
-
-    y = jnp.dot(weight_ref[...], all_feat[...], preferred_element_type=F32)
-    got_ref[0] = y.astype(BF16)
-    y_copies = []
-    for j in range(1, pairs + 1):
-        c = to_dom(got_ref.at[0], got_ref.at[2 * j], y_sem, j - 1, dom_at(2 * j))
-        c.start()
-        y_copies.append(c)
 
     w_term = lax.dot_general(
         all_grad[my_rows], all_feat[...], (((1,), (1,)), ((), ())), preferred_element_type=F32
     )
     for i in range(n_red):
-        w_part[i] = w_term[8 * i:8 * i + 8]
+        w_part[i] = w_term[PIECE * i:PIECE * i + PIECE].astype(BF16)
 
     def when(cond, run):
         if cond is None:
@@ -244,15 +255,16 @@
         else:
             pl.when(cond)(run)
 
+    stride = n_dom // n_red
+
     def reducer(index):
-        return None if n_red == n_dom else index < n_red
-
-    my_piece = me if n_red == n_dom else lax.rem(me, n_red)
+        return None if stride == 1 else lax.rem(index, stride) == 0
+
+    my_piece = lax.div(me, stride)
 
     def rs_copy(k):
         there = dom_at(k)
-        piece = there if n_red == n_dom else lax.rem(there, n_red)
-        return to_dom(w_part.at[piece], pieces.at[me], rs_sem, k - 1, there)
+        return to_dom(w_part.at[lax.div(there, stride)], pieces.at[me], rs_sem, k - 1, there)
 
     def ag_copy(k):
         return to_dom(wgrad_t.at[my_piece], wgrad_t.at[my_piece], ag_sem, k - 1, dom_at(k))
@@ -265,24 +277,27 @@
         lax.fori_loop(1, n_dom, step, 0)
 
     each(lambda k: when(reducer(dom_at(k)), lambda: rs_copy(k).start()))
-    ye_copy = to_dom(got_ref.at[0], got_ref.at[y_extra], ye_sem, 0, dom_at(y_extra))
-    ye_copy.start()
     g_forward()
 
     def reduce_piece():
         pieces[me] = w_part[my_piece]
         each(lambda k: rs_copy(k).wait_recv())
-        wgrad_t[my_piece] = jnp.sum(pieces[...], axis=0) * scale
+        wgrad_t[my_piece] = (jnp.sum(pieces[...].astype(F32), axis=0) * scale).astype(BF16)
         each(lambda k: ag_copy(k).start())
 
     when(reducer(me), reduce_piece)
 
     yf_copies = []
-    for j in range(1, pairs + 1):
-        y_copies[j - 1].wait_recv()
-        c = to_dom(got_ref.at[2 * j], got_ref.at[2 * j + 1 - 2 * odd], yf_sem, j - 1, sib)
-        c.start()
-        yf_copies.append(c)
+    for i in range(CUTS):
+        cols = pl.ds(i * cut, cut)
+        for j in range(1, pairs + 1):
+            y_copies[j - 1][i].wait_recv()
+            c = to_dom(
+                got_ref.at[2 * j, :, cols], got_ref.at[2 * j + 1 - 2 * odd, :, cols],
+                yf_sem, (j - 1) * CUTS + i, sib,
+            )
+            c.start()
+            yf_copies.append(c)
 
     for c in w_copies:
         c.wait_recv()
@@ -291,11 +306,11 @@
     fgrad_ref[...] = jnp.dot(w_mine, all_grad[...], preferred_element_type=F32).astype(BF16)
 
     each(lambda k: when(reducer(dom_at(-k)), lambda: ag_copy(k).wait_recv()))
-    wgrad_ref[...] = wgrad_t[...].reshape(wgrad_ref.shape)
-
-    for c in yf_copies + [ye_copy]:
+    wgrad_ref[...] = wgrad_t[...].astype(F32).reshape(wgrad_ref.shape)
+
+    for c in yf_copies + ye_copies:
         c.wait_recv()
-    for c in sib_copies + w_copies + far_copies + [ex_copy] + y_copies + [ye_copy] + yf_copies:
+    for c in sib_copies + w_copies + far_copies + [ex_copy] + sum(y_copies, []) + ye_copies + yf_copies:
         c.wait_send()
     f_sent()
     g_sent()
@@ -331,12 +346,12 @@
             pltpu.SemaphoreType.DMA((4,)),
             pltpu.SemaphoreType.DMA((steps,)),
         ],
-        compiler_params=pltpu.CompilerParams(vmem_limit_bytes=VMEM_LIMIT),
+        compiler_params=pltpu.CompilerParams(vmem_limit_bytes=PULL_LIMIT),
         name="pull",
     )(row_tiles, col_tiles, tile_counts, cotangent_t, values)
 
     pairs = steps // 2 - 1
-    n_red = min(width // 8, n_dom)
+    n_red = min(width // PIECE, n_dom)
 
     def sems(count):
         return pltpu.SemaphoreType.DMA((2, count))
@@ -358,13 +373,13 @@
             pltpu.VMEM((pairs, width, nodes), BF16),
             pltpu.VMEM((pairs, width, nodes), BF16),
             pltpu.VMEM((width, nodes), BF16),
-            pltpu.VMEM((n_dom, 8, hid), F32),
-            pltpu.VMEM((n_red, 8, hid), F32),
-            pltpu.VMEM((n_red, 8, hid), F32),
+            pltpu.VMEM((n_dom, PIECE, hid), BF16),
+            pltpu.VMEM((n_red, PIECE, hid), BF16),
+            pltpu.VMEM((n_red, PIECE, hid), BF16),
             pltpu.VMEM((n_feat, width, width), BF16),
             sems(2 * n_feat - 2), sems(n_feat - 1), sems(2 * n_feat - 2),
             sems(pairs), sems(pairs), sems(1),
-            sems(pairs), sems(pairs), sems(1),
+            sems(pairs * CUTS), sems(pairs * CUTS), sems(CUTS),
             sems(n_dom - 1), sems(n_dom - 1),
         ],
         compiler_params=pltpu.CompilerParams(

time: 42.2 us -> 44.9 us (1.064)
  Pallas kernels: 34.6 us -> 38.9 us
  local copies, waits for them, and re-layouts: 6.59 us -> 5.03 us
    pallas_call x1, Pallas kernels: 29.3 us -> 31.8 us  [body(): pl.pallas_call(functools.partial(exchange_kernel, n_dom, n_feat, 1.0 / ma...]
    pallas_call x1, Pallas kernels: 2.06 us -> 3.9 us  [body(): pl.pallas_call(pull_kernel, out_shape=(jax.ShapeDtypeStruct((steps, width...]
    unnamed x18, local copies, waits for them, and re-layouts: 6.59 us -> 5.03 us
where the time goes in v3:
time: 44.9 us; the launch traced here: 44.7 us
  Pallas kernels  38.9 us (87%)
  local copies, waits for them, and re-layouts  5.03 us (11%)
  between operations  0.75 us (2%)
    pallas_call x1, Pallas kernels, body(): pl.pallas_call(functools.partial(exchange_kernel, n_dom, n_feat, 1.0 / ma...  31.8 us
    unnamed x18, local copies, waits for them, and re-layouts  5.03 us
    pallas_call x1, Pallas kernels, body(): pl.pallas_call(pull_kernel, out_shape=(jax.ShapeDtypeStruct((steps, width...  3.9 us
    pallas_call x1, Pallas kernels, body(): pl.pallas_call(push_kernel, out_shape=jax.ShapeDtypeStruct((width, nodes)...  3.2 us

profile of v3, /device:TPU:0, one launch (start us, length us, event | category | flops | bytes accessed | tf_op | source)
XLA Modules:
  0.0 44.7 jit_solution(15744055060754846439)
XLA Ops:
  0.6 0.0 copy-start.7
  0.6 0.0 copy-start.6
  0.7 0.0 copy-start.5
  0.7 0.0 copy-start.4
  0.7 0.0 copy-start.3
  0.7 3.9 %pull.1 = (bf16[4,64,1536]{2,1,0:T(8,128)(2,1)}, f32[64,1536]{1,0:T(8,128)}) custom-call(s32[1,4,16]{2,1,0:T(4,128)} %row_ref.1, s32[1,4,16]{2,1,0:T(4,128)} %col_ref.1, s32[1,4]{1,0:T(1,128)} %count_ref.1, bf16[64,1536]{1,0:T(8,128)(2,1)} %cot_hbm.1, bf16[4,16,128,128]{3,2,1,0:T(8,128)(2,1)} %bitcast.3), custom_call_target="tpu_custom_call" | custom-call | tf_op jit(solution)/shard_map/pull/pallas_call | solution.py:331
  4.6 0.0 copy-done.4
  4.6 0.0 copy-done.3
  4.6 0.0 copy-start.1
  4.6 1.1 %copy-done.1 = bf16[4,64,1536]{2,1,0:T(8,128)(2,1)S(1)} copy-done((bf16[4,64,1536]{2,1,0:T(8,128)(2,1)S(1)}, bf16[4,64,1536]{2,1,0:T(8,128)(2,1)}, u32[]{:S(2)}) %copy-start.1) | copy-done | bytes 786456
  5.7 0.0 copy-start.2
  5.7 1.0 %copy-done.2 = f32[64,1536]{1,0:T(8,128)S(1)} copy-done((f32[64,1536]{1,0:T(8,128)S(1)}, f32[64,1536]{1,0:T(8,128)}, u32[]{:S(2)}) %copy-start.2) | copy-done | bytes 393240
  6.7 31.8 %exchange.1 = (bf16[4,64,1536]{2,1,0:T(8,128)(2,1)S(1)}, f32[64,256]{1,0:T(8,128)S(1)}, bf16[64,1536]{1,0:T(8,128)(2,1)S(1)}) custom-call(bf16[64,1536]{1,0:T(8,128)(2,1)S(1)} %copy-done.3, bf16[64,256]{1,0:T(8,128)(2,1)S(1)} %bitcast.6, bf16[4,64,1536]{2,1,0:T(8,128)(2,1)S(1)} %copy-done.1, f32[64,1536]{1,0:T(8,128)S(1)} %copy-done.2), custom_call_target="tpu_custom_call" | custom-call | tf_op jit(solution)/shard_map/exchange/pallas_call | solution.py:359
  38.5 0.0 copy-done.7
  38.5 0.0 copy-done.6
  38.5 0.0 copy-done.5
  38.6 0.0 copy-start
  38.6 1.6 %copy-done = bf16[1,4,16,128,128]{4,3,2,1,0:T(8,128)(2,1)S(1)} copy-done((bf16[1,4,16,128,128]{4,3,2,1,0:T(8,128)(2,1)S(1)}, bf16[1,4,16,128,128]{4,3,2,1,0:T(8,128)(2,1)}, u32[]{:S(2)}) %copy-start) | copy-done | bytes 2097176
  40.1 3.2 %push.1 = bf16[64,1536]{1,0:T(8,128)(2,1)} custom-call(s32[1,4,16]{2,1,0:T(4,128)S(1)} %copy-done.5, s32[1,4,16]{2,1,0:T(4,128)S(1)} %copy-done.6, s32[1,4]{1,0:T(1,128)S(1)} %copy-done.7, bf16[4,64,1536]{2,1,0:T(8,128)(2,1)S(1)} %get-tuple-element.10.got_ref, bf16[4,16,128,128]{3,2,1,0:T(8,128)(2,1)S(1)} %bitcast.4), custom_call_target="tpu_custom_call" | custom-call | tf_op jit(solution)/shard_map/push/pallas_call | solution.py:391
  43.3 0.6 %copy.12 = f32[256,64]{0,1:T(8,128)} copy(f32[256,64]{0,1:T(8,128)S(1)} %bitcast.5) | data formatting | bytes 131072
  44.0 0.7 %copy.13 = bf16[64,1536]{1,0:T(8,128)(2,1)} copy(bf16[64,1536]{1,0:T(8,128)(2,1)S(1)} %get-tuple-element.18) | data formatting | bytes 393216
Async XLA Ops:
  0.6 37.9 %copy-start.7 = (s32[1,4]{1,0:T(1,128)S(1)}, s32[1,4]{1,0:T(1,128)}, u32[]{:S(2)}) copy-start(s32[1,4]{1,0:T(1,128)} %count_ref.1) | copy-start | bytes 52
  0.6 37.9 %copy-start.6 = (s32[1,4,16]{2,1,0:T(4,128)S(1)}, s32[1,4,16]{2,1,0:T(4,128)}, u32[]{:S(2)}) copy-start(s32[1,4,16]{2,1,0:T(4,128)} %col_ref.1) | copy-start | bytes 772
  0.7 37.9 %copy-start.5 = (s32[1,4,16]{2,1,0:T(4,128)S(1)}, s32[1,4,16]{2,1,0:T(4,128)}, u32[]{:S(2)}) copy-start(s32[1,4,16]{2,1,0:T(4,128)} %row_ref.1) | copy-start | bytes 772
  0.7 3.9 %copy-start.4 = (bf16[256,64]{0,1:T(8,128)(2,1)S(1)}, bf16[256,64]{0,1:T(8,128)(2,1)}, u32[]{:S(2)}) copy-start(bf16[256,64]{0,1:T(8,128)(2,1)} %param.8) | copy-start | bytes 98308
  0.7 3.9 %copy-start.3 = (bf16[64,1536]{1,0:T(8,128)(2,1)S(1)}, bf16[64,1536]{1,0:T(8,128)(2,1)}, u32[]{:S(2)}) copy-start(bf16[64,1536]{1,0:T(8,128)(2,1)} %feat_ref.1) | copy-start | bytes 589828
  4.6 1.1 %copy-start.1 = (bf16[4,64,1536]{2,1,0:T(8,128)(2,1)S(1)}, bf16[4,64,1536]{2,1,0:T(8,128)(2,1)}, u32[]{:S(2)}) copy-start(bf16[4,64,1536]{2,1,0:T(8,128)(2,1)} %get-tuple-element.8.part_ref) | copy-start | bytes 2359300
  5.7 1.0 %copy-start.2 = (f32[64,1536]{1,0:T(8,128)S(1)}, f32[64,1536]{1,0:T(8,128)}, u32[]{:S(2)}) copy-start(f32[64,1536]{1,0:T(8,128)} %get-tuple-element.9.own_ref) | copy-start | bytes 1179652
  38.6 1.6 %copy-start = (bf16[1,4,16,128,128]{4,3,2,1,0:T(8,128)(2,1)S(1)}, bf16[1,4,16,128,128]{4,3,2,1,0:T(8,128)(2,1)}, u32[]{:S(2)}) copy-start(bf16[1,4,16,128,128]{4,3,2,1,0:T(8,128)(2,1)} %param.9) | copy-start | bytes 6291460

commit v4 on v3

--- a/solution.py
+++ b/solution.py
@@ -13,7 +13,7 @@
 BF16 = jnp.bfloat16
 VMEM_LIMIT = 40 * 1024 * 1024
 PULL_LIMIT = 62 * 1024 * 1024
-CUTS = 3
+CUTS = 1
 PIECE = 16
 
 
@@ -22,7 +22,7 @@
 
 
 def pull_kernel(
-    row_hbm, col_hbm, count_hbm, cot_hbm, val_hbm, part_ref, own_ref,
+    row_hbm, col_hbm, count_hbm, cot_hbm, val_hbm, part_ref,
     row_ref, col_ref, count_ref, cot_ref, val_ref, acc, sem, val_sem,
 ):
     steps, slots, side = val_ref.shape[0], val_ref.shape[1], val_ref.shape[3]
@@ -58,11 +58,6 @@
             acc[:, lanes(target, side)] += term
         total = acc[:, :nodes]
         part_ref[s] = total.astype(BF16)
-
-        @pl.when(s == 0)
-        def _():
-            own_ref[...] = total
-
         return carry
 
     lax.fori_loop(0, steps, one, 0)
@@ -92,7 +87,7 @@
 
 def exchange_kernel(
     n_dom, n_feat, scale,
-    feat_ref, weight_ref, part_ref, own_ref,
+    feat_ref, weight_ref, part_ref,
     got_ref, wgrad_ref, fgrad_ref,
     all_feat, all_grad, w_cols, sib_part, sum_part, far_part, extra_part, pieces, wgrad_t,
     w_part, w_out, f_sem, w_sem, g_sem, sib_sem, far_sem, ex_sem, y_sem, yf_sem, ye_sem, rs_sem, ag_sem,
@@ -105,7 +100,6 @@
     odd = lax.rem(me, 2)
     sib = me + 1 - 2 * odd
     extra = jnp.where(odd == 1, 1, steps - 1)
-    y_extra = jnp.where(odd == 1, steps - 1, 1)
 
     def dom_at(offset):
         return lax.rem(me + offset + n_dom, n_dom)
@@ -193,8 +187,6 @@
         c = to_dom(part_ref.at[2 * j - 1 + 2 * odd], sib_part.at[j - 1], sib_sem, j - 1, sib)
         c.start()
         sib_copies.append(c)
-    ex_copy = to_dom(part_ref.at[extra], extra_part, ex_sem, 0, dom_at(-extra))
-    ex_copy.start()
     all_feat[my_rows] = feat_ref[...]
     f_begin, f_forward, f_arrive, f_sent = gather(all_feat, f_sem)
     g_begin, g_forward, g_arrive, g_sent = gather(all_grad, g_sem)
@@ -206,6 +198,8 @@
         c = to_dom(sum_part.at[j - 1], far_part.at[j - 1], far_sem, j - 1, dom_at(-2 * j))
         c.start()
         far_copies.append(c)
+    ex_copy = to_dom(part_ref.at[extra], extra_part, ex_sem, 0, dom_at(-extra))
+    ex_copy.start()
     weight = weight_ref[...].T
     for k in range(n_feat):
         w_out[k] = weight[k * width:(k + 1) * width]
@@ -219,29 +213,25 @@
 
     cut = nodes // CUTS
     y_copies = [[] for _ in range(pairs)]
-    ye_copies = []
-    f_arrive()
-    for i in range(CUTS):
-        cols = pl.ds(i * cut, cut)
-        y = jnp.dot(weight_ref[...], all_feat[:, cols], preferred_element_type=F32)
-        got_ref[0, :, cols] = y.astype(BF16)
-        here = got_ref.at[0, :, cols]
-        c = to_dom(here, got_ref.at[y_extra, :, cols], ye_sem, i, dom_at(y_extra))
-        c.start()
-        ye_copies.append(c)
-        for j in range(1, pairs + 1):
-            c = to_dom(here, got_ref.at[2 * j, :, cols], y_sem, (j - 1) * CUTS + i, dom_at(2 * j))
-            c.start()
-            y_copies[j - 1].append(c)
-
-    total = own_ref[...]
+    total = part_ref[0].astype(F32)
     ex_copy.wait_recv()
     total += extra_part[...].astype(F32)
     for j in range(1, pairs + 1):
         far_copies[j - 1].wait_recv()
         total += far_part[j - 1].astype(F32)
     all_grad[my_rows] = total.astype(BF16)
+
+    f_arrive()
     g_begin()
+    for i in range(CUTS):
+        cols = pl.ds(i * cut, cut)
+        y = jnp.dot(weight_ref[...], all_feat[:, cols], preferred_element_type=F32)
+        got_ref[0, :, cols] = y.astype(BF16)
+        here = got_ref.at[0, :, cols]
+        for j in range(1, pairs + 1):
+            c = to_dom(here, got_ref.at[2 * j, :, cols], y_sem, (j - 1) * CUTS + i, dom_at(2 * j))
+            c.start()
+            y_copies[j - 1].append(c)
 
     w_term = lax.dot_general(
         all_grad[my_rows], all_feat[...], (((1,), (1,)), ((), ())), preferred_element_type=F32
@@ -299,6 +289,10 @@
             c.start()
             yf_copies.append(c)
 
+    ye_from = jnp.where(odd == 1, steps - 2, 0)
+    ye_copies = [to_dom(got_ref.at[ye_from], got_ref.at[ye_from + 1], ye_sem, 0, dom_at(1))]
+    ye_copies[0].start()
+
     for c in w_copies:
         c.wait_recv()
     w_mine = jnp.concatenate([w_cols[k] for k in range(n_feat)], axis=1)
@@ -328,14 +322,11 @@
     hbm = pl.BlockSpec(memory_space=pltpu.HBM)
     acc = pltpu.VMEM((width, nodes + side), F32)
 
-    part, own = pl.pallas_call(
+    part = pl.pallas_call(
         pull_kernel,
-        out_shape=(
-            jax.ShapeDtypeStruct((steps, width, nodes), BF16),
-            jax.ShapeDtypeStruct((width, nodes), F32),
-        ),
+        out_shape=jax.ShapeDtypeStruct((steps, width, nodes), BF16),
         in_specs=[hbm] * 5,
-        out_specs=(vmem, vmem),
+        out_specs=vmem,
         scratch_shapes=[
             pltpu.SMEM(row_tiles.shape, jnp.int32),
             pltpu.SMEM(col_tiles.shape, jnp.int32),
@@ -363,7 +354,7 @@
             jax.ShapeDtypeStruct((width, hid), F32),
             jax.ShapeDtypeStruct((width, nodes), BF16),
         ),
-        in_specs=[vmem] * 4,
+        in_specs=[vmem] * 3,
         out_specs=(vmem,) * 3,
         scratch_shapes=[
             pltpu.VMEM((hid, nodes), BF16),
@@ -386,7 +377,7 @@
             vmem_limit_bytes=VMEM_LIMIT, collective_id=0, has_side_effects=True
         ),
         name="exchange",
-    )(features_t, weight.T, part, own)
+    )(features_t, weight.T, part)
 
     output_t = pl.pallas_call(
         push_kernel,

time: 44.9 us -> 39.6 us (0.88)
  Pallas kernels: 38.9 us -> 34.6 us
  local copies, waits for them, and re-layouts: 5.03 us -> 4.04 us
    pallas_call x1, Pallas kernels: 31.8 us -> 27.7 us  [body(): pl.pallas_call(functools.partial(exchange_kernel, n_dom, n_feat, 1.0 / ma...]
    unnamed x18 -> x16, local copies, waits for them, and re-layouts: 5.03 us -> 4.04 us
where the time goes in v4:
time: 39.6 us; the launch traced here: 39.4 us
  Pallas kernels  34.6 us (87%)
  local copies, waits for them, and re-layouts  4.04 us (10%)
  between operations  0.74 us (2%)
    pallas_call x1, Pallas kernels, body(): pl.pallas_call(functools.partial(exchange_kernel, n_dom, n_feat, 1.0 / ma...  27.7 us
    unnamed x16, local copies, waits for them, and re-layouts  4.04 us
    pallas_call x1, Pallas kernels, body(): pl.pallas_call(pull_kernel, out_shape=jax.ShapeDtypeStruct((steps, width,...  3.72 us
    pallas_call x1, Pallas kernels, body(): pl.pallas_call(push_kernel, out_shape=jax.ShapeDtypeStruct((width, nodes)...  3.2 us

profile of v4, /device:TPU:0, one launch (start us, length us, event | category | flops | bytes accessed | tf_op | source)
XLA Modules:
  0.0 39.4 jit_solution(16954362487305935900)
XLA Ops:
  0.6 0.0 copy-start.6
  0.6 0.0 copy-start.5
  0.7 0.0 copy-start.4
  0.7 0.0 copy-start.3
  0.7 0.0 copy-start.2
  0.7 3.7 %pull.1.part_ref = bf16[4,64,1536]{2,1,0:T(8,128)(2,1)} custom-call(s32[1,4,16]{2,1,0:T(4,128)} %row_ref.1, s32[1,4,16]{2,1,0:T(4,128)} %col_ref.1, s32[1,4]{1,0:T(1,128)} %count_ref.1, bf16[64,1536]{1,0:T(8,128)(2,1)} %cot_hbm.1, bf16[4,16,128,128]{3,2,1,0:T(8,128)(2,1)} %bitcast.3), custom_call_target="tpu_custom_call" | custom-call | tf_op jit(solution)/shard_map/pull/pallas_call | solution.py:325
  4.4 0.0 copy-done.3
  4.4 0.0 copy-done.2
  4.4 0.0 copy-start.1
  4.4 1.1 %copy-done.1 = bf16[4,64,1536]{2,1,0:T(8,128)(2,1)S(1)} copy-done((bf16[4,64,1536]{2,1,0:T(8,128)(2,1)S(1)}, bf16[4,64,1536]{2,1,0:T(8,128)(2,1)}, u32[]{:S(2)}) %copy-start.1) | copy-done | bytes 786456
  5.6 27.7 %exchange.1 = (bf16[4,64,1536]{2,1,0:T(8,128)(2,1)S(1)}, f32[64,256]{1,0:T(8,128)S(1)}, bf16[64,1536]{1,0:T(8,128)(2,1)S(1)}) custom-call(bf16[64,1536]{1,0:T(8,128)(2,1)S(1)} %copy-done.2, bf16[64,256]{1,0:T(8,128)(2,1)S(1)} %bitcast.6, bf16[4,64,1536]{2,1,0:T(8,128)(2,1)S(1)} %copy-done.1), custom_call_target="tpu_custom_call" | custom-call | tf_op jit(solution)/shard_map/exchange/pallas_call | solution.py:350
  33.3 0.0 copy-done.6
  33.3 0.0 copy-done.5
  33.3 0.0 copy-done.4
  33.3 0.0 copy-start
  33.3 1.6 %copy-done = bf16[1,4,16,128,128]{4,3,2,1,0:T(8,128)(2,1)S(1)} copy-done((bf16[1,4,16,128,128]{4,3,2,1,0:T(8,128)(2,1)S(1)}, bf16[1,4,16,128,128]{4,3,2,1,0:T(8,128)(2,1)}, u32[]{:S(2)}) %copy-start) | copy-done | bytes 2097176
  34.9 3.2 %push.1 = bf16[64,1536]{1,0:T(8,128)(2,1)} custom-call(s32[1,4,16]{2,1,0:T(4,128)S(1)} %copy-done.4, s32[1,4,16]{2,1,0:T(4,128)S(1)} %copy-done.5, s32[1,4]{1,0:T(1,128)S(1)} %copy-done.6, bf16[4,64,1536]{2,1,0:T(8,128)(2,1)S(1)} %get-tuple-element.6.got_ref, bf16[4,16,128,128]{3,2,1,0:T(8,128)(2,1)S(1)} %bitcast.4), custom_call_target="tpu_custom_call" | custom-call | tf_op jit(solution)/shard_map/push/pallas_call | solution.py:382
  38.1 0.6 %copy.12 = f32[256,64]{0,1:T(8,128)} copy(f32[256,64]{0,1:T(8,128)S(1)} %bitcast.5) | data formatting | bytes 131072
  38.7 0.7 %copy.13 = bf16[64,1536]{1,0:T(8,128)(2,1)} copy(bf16[64,1536]{1,0:T(8,128)(2,1)S(1)} %get-tuple-element.14) | data formatting | bytes 393216
Async XLA Ops:
  0.6 32.7 %copy-start.6 = (s32[1,4]{1,0:T(1,128)S(1)}, s32[1,4]{1,0:T(1,128)}, u32[]{:S(2)}) copy-start(s32[1,4]{1,0:T(1,128)} %count_ref.1) | copy-start | bytes 52
  0.6 32.7 %copy-start.5 = (s32[1,4,16]{2,1,0:T(4,128)S(1)}, s32[1,4,16]{2,1,0:T(4,128)}, u32[]{:S(2)}) copy-start(s32[1,4,16]{2,1,0:T(4,128)} %col_ref.1) | copy-start | bytes 772
  0.7 32.7 %copy-start.4 = (s32[1,4,16]{2,1,0:T(4,128)S(1)}, s32[1,4,16]{2,1,0:T(4,128)}, u32[]{:S(2)}) copy-start(s32[1,4,16]{2,1,0:T(4,128)} %row_ref.1) | copy-start | bytes 772
  0.7 3.7 %copy-start.3 = (bf16[256,64]{0,1:T(8,128)(2,1)S(1)}, bf16[256,64]{0,1:T(8,128)(2,1)}, u32[]{:S(2)}) copy-start(bf16[256,64]{0,1:T(8,128)(2,1)} %param.8) | copy-start | bytes 98308
  0.7 3.7 %copy-start.2 = (bf16[64,1536]{1,0:T(8,128)(2,1)S(1)}, bf16[64,1536]{1,0:T(8,128)(2,1)}, u32[]{:S(2)}) copy-start(bf16[64,1536]{1,0:T(8,128)(2,1)} %feat_ref.1) | copy-start | bytes 589828
  4.4 1.1 %copy-start.1 = (bf16[4,64,1536]{2,1,0:T(8,128)(2,1)S(1)}, bf16[4,64,1536]{2,1,0:T(8,128)(2,1)}, u32[]{:S(2)}) copy-start(bf16[4,64,1536]{2,1,0:T(8,128)(2,1)} %pull.1.part_ref) | copy-start | bytes 2359300
  33.3 1.6 %copy-start = (bf16[1,4,16,128,128]{4,3,2,1,0:T(8,128)(2,1)S(1)}, bf16[1,4,16,128,128]{4,3,2,1,0:T(8,128)(2,1)}, u32[]{:S(2)}) copy-start(bf16[1,4,16,128,128]{4,3,2,1,0:T(8,128)(2,1)} %param.9) | copy-start | bytes 6291460

commit v5 on v4

--- a/solution.py
+++ b/solution.py
@@ -12,7 +12,7 @@
 F32 = jnp.float32
 BF16 = jnp.bfloat16
 VMEM_LIMIT = 40 * 1024 * 1024
-PULL_LIMIT = 62 * 1024 * 1024
+PULL_LIMIT = 58 * 1024 * 1024
 CUTS = 1
 PIECE = 16
 

time: 39.6 us -> 38.1 us (0.962)
  local copies, waits for them, and re-layouts: 4.04 us -> 2.46 us
    unnamed x16, local copies, waits for them, and re-layouts: 4.04 us -> 2.46 us
where the time goes in v5:
time: 38.1 us; the launch traced here: 38 us
  Pallas kernels  34.7 us (91%)
  local copies, waits for them, and re-layouts  2.46 us (6%)
  between operations  0.75 us (2%)
    pallas_call x1, Pallas kernels, body(): pl.pallas_call(functools.partial(exchange_kernel, n_dom, n_feat, 1.0 / ma...  27.7 us
    pallas_call x1, Pallas kernels, body(): pl.pallas_call(pull_kernel, out_shape=jax.ShapeDtypeStruct((steps, width,...  3.83 us
    pallas_call x1, Pallas kernels, body(): pl.pallas_call(push_kernel, out_shape=jax.ShapeDtypeStruct((width, nodes)...  3.2 us
    unnamed x16, local copies, waits for them, and re-layouts  2.46 us

profile of v5, /device:TPU:0, one launch (start us, length us, event | category | flops | bytes accessed | tf_op | source)
XLA Modules:
  0.0 38.0 jit_solution(2471199548777026801)
XLA Ops:
  0.6 0.0 copy-start.6
  0.6 0.0 copy-start.5
  0.7 0.0 copy-start.4
  0.7 0.0 copy-start
  0.7 0.0 copy-start.3
  0.7 0.0 copy-start.2
  0.7 3.8 %pull.1.part_ref = bf16[4,64,1536]{2,1,0:T(8,128)(2,1)} custom-call(s32[1,4,16]{2,1,0:T(4,128)} %row_ref.1, s32[1,4,16]{2,1,0:T(4,128)} %col_ref.1, s32[1,4]{1,0:T(1,128)} %count_ref.1, bf16[64,1536]{1,0:T(8,128)(2,1)} %cot_hbm.1, bf16[4,16,128,128]{3,2,1,0:T(8,128)(2,1)} %bitcast.3), custom_call_target="tpu_custom_call" | custom-call | tf_op jit(solution)/shard_map/pull/pallas_call | solution.py:325
  4.5 0.0 copy-done.3
  4.5 0.0 copy-done.2
  4.6 0.0 copy-start.1
  4.6 1.1 %copy-done.1 = bf16[4,64,1536]{2,1,0:T(8,128)(2,1)S(1)} copy-done((bf16[4,64,1536]{2,1,0:T(8,128)(2,1)S(1)}, bf16[4,64,1536]{2,1,0:T(8,128)(2,1)}, u32[]{:S(2)}) %copy-start.1) | copy-done | bytes 786456
  5.7 27.7 %exchange.1 = (bf16[4,64,1536]{2,1,0:T(8,128)(2,1)S(1)}, f32[64,256]{1,0:T(8,128)S(1)}, bf16[64,1536]{1,0:T(8,128)(2,1)S(1)}) custom-call(bf16[64,1536]{1,0:T(8,128)(2,1)S(1)} %copy-done.2, bf16[64,256]{1,0:T(8,128)(2,1)S(1)} %bitcast.6, bf16[4,64,1536]{2,1,0:T(8,128)(2,1)S(1)} %copy-done.1), custom_call_target="tpu_custom_call" | custom-call | tf_op jit(solution)/shard_map/exchange/pallas_call | solution.py:350
  33.4 0.0 copy-done.6
  33.4 0.0 copy-done.5
  33.4 0.0 copy-done.4
  33.4 0.0 copy-done
  33.4 3.2 %push.1 = bf16[64,1536]{1,0:T(8,128)(2,1)} custom-call(s32[1,4,16]{2,1,0:T(4,128)S(1)} %copy-done.4, s32[1,4,16]{2,1,0:T(4,128)S(1)} %copy-done.5, s32[1,4]{1,0:T(1,128)S(1)} %copy-done.6, bf16[4,64,1536]{2,1,0:T(8,128)(2,1)S(1)} %get-tuple-element.6.got_ref, bf16[4,16,128,128]{3,2,1,0:T(8,128)(2,1)S(1)} %bitcast.4), custom_call_target="tpu_custom_call" | custom-call | tf_op jit(solution)/shard_map/push/pallas_call | solution.py:382
  36.6 0.6 %copy.12 = f32[256,64]{0,1:T(8,128)} copy(f32[256,64]{0,1:T(8,128)S(1)} %bitcast.5) | data formatting | bytes 131072
  37.3 0.7 %copy.13 = bf16[64,1536]{1,0:T(8,128)(2,1)} copy(bf16[64,1536]{1,0:T(8,128)(2,1)S(1)} %get-tuple-element.14) | data formatting | bytes 393216
Async XLA Ops:
  0.6 32.8 %copy-start.6 = (s32[1,4]{1,0:T(1,128)S(1)}, s32[1,4]{1,0:T(1,128)}, u32[]{:S(2)}) copy-start(s32[1,4]{1,0:T(1,128)} %count_ref.1) | copy-start | bytes 52
  0.6 32.8 %copy-start.5 = (s32[1,4,16]{2,1,0:T(4,128)S(1)}, s32[1,4,16]{2,1,0:T(4,128)}, u32[]{:S(2)}) copy-start(s32[1,4,16]{2,1,0:T(4,128)} %col_ref.1) | copy-start | bytes 772
  0.7 32.8 %copy-start.4 = (s32[1,4,16]{2,1,0:T(4,128)S(1)}, s32[1,4,16]{2,1,0:T(4,128)}, u32[]{:S(2)}) copy-start(s32[1,4,16]{2,1,0:T(4,128)} %row_ref.1) | copy-start | bytes 772
  0.7 32.8 %copy-start = (bf16[1,4,16,128,128]{4,3,2,1,0:T(8,128)(2,1)S(1)}, bf16[1,4,16,128,128]{4,3,2,1,0:T(8,128)(2,1)}, u32[]{:S(2)}) copy-start(bf16[1,4,16,128,128]{4,3,2,1,0:T(8,128)(2,1)} %param.9) | copy-start | bytes 6291460
  0.7 3.9 %copy-start.3 = (bf16[256,64]{0,1:T(8,128)(2,1)S(1)}, bf16[256,64]{0,1:T(8,128)(2,1)}, u32[]{:S(2)}) copy-start(bf16[256,64]{0,1:T(8,128)(2,1)} %param.8) | copy-start | bytes 98308
  0.7 3.9 %copy-start.2 = (bf16[64,1536]{1,0:T(8,128)(2,1)S(1)}, bf16[64,1536]{1,0:T(8,128)(2,1)}, u32[]{:S(2)}) copy-start(bf16[64,1536]{1,0:T(8,128)(2,1)} %feat_ref.1) | copy-start | bytes 589828
  4.6 1.1 %copy-start.1 = (bf16[4,64,1536]{2,1,0:T(8,128)(2,1)S(1)}, bf16[4,64,1536]{2,1,0:T(8,128)(2,1)}, u32[]{:S(2)}) copy-start(bf16[4,64,1536]{2,1,0:T(8,128)(2,1)} %pull.1.part_ref) | copy-start | bytes 2359300
